TPU v7x, 32 devices: a whole 2x2x4 slice. The times are simulated.
32 devices in a mesh: chan: 16 (over z, x, core), tm: 2 (over y).
Axes of the slice: x: 2, y: 2, z: 4, core: 2. Of those that a mesh axis runs over, the one named last changes fastest.
Arguments:
- records: bfloat16 [1024, 65536], P('chan', 'tm'), may hold values from -6 to 6
- coords: int32 [2, 1024], P(None, 'chan'), may hold values from 0 to 1023
- bins: int32 [256], replicated, may hold values from 1 to 1023
- slow_index: int32 [2, 2048], replicated, may hold values from -32 to 32
Outputs:
- beam_power: float32 [2048, 256], P('tm', 'chan')
All inputs are finite; a program needn't handle non-finite values.
Results may differ from a plain program's by a relative error of at most 0.0011.
Values may be sent and summed in bfloat16 or wider, within the bound.
A program may use at most 64 MiB of HBM per device.

v0:
```python
import math

import jax
import jax.numpy as jnp
from jax import lax
from jax.sharding import PartitionSpec as P

W = 2048


def shifted(block, axis, distance):
    devices = range(lax.axis_size(axis))
    route = [(i - distance, i) for i in devices if i - distance in devices]
    return lax.ppermute(block, axis, route)


def taper_table(bins, width):
    offsets = jnp.arange(width, dtype=jnp.int32)
    turns = jnp.remainder(bins[None, :] * offsets[:, None], width).astype(jnp.float32) * (
        2.0 * math.pi / width
    )
    taper = 0.5 - 0.5 * jnp.cos(offsets.astype(jnp.float32) * (2.0 * math.pi / width))
    weight = (taper * math.sqrt(8.0 / (3.0 * width)))[:, None]
    table = jnp.stack([weight * jnp.cos(turns), -weight * jnp.sin(turns)], axis=-1)
    return table.reshape(width, -1).astype(jnp.bfloat16)


def replica_rows(delay, bin_value, width):
    modulus = 5 * width
    phase = jnp.remainder(2 * bin_value * delay, modulus).astype(jnp.float32) * (
        2.0 * math.pi / modulus
    )
    return jnp.concatenate([jnp.cos(phase), jnp.sin(phase)], axis=0).astype(jnp.bfloat16)


def beam_rows(start, count, received, bins, bin_base, positions, slow_index, scale):
    bin_count, _, groups, chan_count, snaps_dev, ch_dev = received.shape
    block = math.gcd(count, 512)

    def beam_block(first_row):
        rows = lax.dynamic_slice_in_dim(slow_index, first_row, block, 1)
        delay = rows[0][:, None] * positions[0][None, :] + rows[1][:, None] * positions[1][None, :]
        columns = []
        for local_bin in range(bin_count):
            bin_value = lax.dynamic_index_in_dim(bins, bin_base + local_bin, keepdims=False)
            replica = replica_rows(delay, bin_value, W).reshape(2 * block, chan_count, ch_dev)
            prod = jnp.einsum(
                "rdc,ptdnc->rptn", replica, received[local_bin], preferred_element_type=jnp.float32
            )
            real_part = prod[:block, 0] + prod[block:, 1]
            imag_part = prod[:block, 1] - prod[block:, 0]
            columns.append(
                jnp.sum(real_part * real_part + imag_part * imag_part, axis=(1, 2)) * scale
            )
        return jnp.stack(columns, axis=1)

    starts = start + block * jnp.arange(count // block, dtype=jnp.int32)
    return lax.map(beam_block, starts).reshape(count, bin_count)


def shards(records, coords, bins, slow_index):
    ch_dev, local_samples = records.shape
    hop = W // 2
    snaps_dev = local_samples // hop
    chan_count = lax.axis_size("chan")
    tm_count = lax.axis_size("tm")
    channels = ch_dev * chan_count
    freq = bins.shape[0]
    slow_count = slow_index.shape[1]
    scale = 1.0 / (channels * snaps_dev * tm_count)
    table = taper_table(bins, W)
    blocks = records.reshape(ch_dev, snaps_dev, hop)
    following = shifted(records[:, :hop], "tm", -1)
    first = jnp.einsum("cnj,jq->qnc", blocks, table[:hop], preferred_element_type=jnp.float32)
    second = jnp.einsum(
        "cnj,jq->qnc", blocks[:, 1:], table[hop:], preferred_element_type=jnp.float32
    )
    tail = jnp.einsum("cj,jq->qc", following, table[hop:], preferred_element_type=jnp.float32)
    second = jnp.concatenate([second, tail[:, None, :]], axis=1)
    spectra = (first + second).astype(jnp.bfloat16).reshape(2 * freq, snaps_dev * ch_dev)
    positions = lax.all_gather(coords, "chan", axis=1, tiled=True)
    received = lax.all_to_all(
        lax.all_to_all(spectra, "chan", split_axis=0, concat_axis=1, tiled=True),
        "tm",
        split_axis=0,
        concat_axis=1,
        tiled=True,
    )
    per_dev = freq // (chan_count * tm_count)
    received = received.reshape(per_dev, 2, tm_count, chan_count, snaps_dev, ch_dev)
    bin_base = (lax.axis_index("chan") * tm_count + lax.axis_index("tm")) * per_dev
    whole = beam_rows(0, slow_count, received, bins, bin_base, positions, slow_index, scale)
    power = lax.all_to_all(whole, "tm", split_axis=0, concat_axis=1, tiled=True)
    return power


def solution(mesh):
    return jax.shard_map(
        shards,
        mesh=mesh,
        in_specs=(P("chan", "tm"), P(None, "chan"), P(), P()),
        out_specs=P("tm", "chan"),
        check_vma=False,
    )
```

profile of v0, /device:TPU:10, one launch (start us, length us, event | category | flops | bytes accessed | tf_op | source)
XLA Modules:
  0.0 492.0 jit_solution(13771937441469708110)
XLA Ops:
  0.0 0.9 slice.288
  0.9 1.3 collective-permute-start
  2.3 9.9 %multiply_convert_fusion.1 = (bf16[2048,256,1]{1,0,2:T(8,128)(2,1)S(1)}, bf16[2048,256,1]{1,0,2:T(8,128)(2,1)S(1)}) fusion(s32[256]{0:T(256)} %param.8, f32[2048]{0:T(1024)S(1)} %get-tuple-element.290, f32[2048]{0:T(1024)S(1)} %get-tuple-element.291), kind=kLoop, calls=%fused_computation.212 | loop fusion | flops 9437184 | bytes 2114560 | tf_op jit(solution)/shard_map/convert.16
  12.3 1.1 copy.25
  13.9 2.6 copy.54
  16.5 4.2 fusion.131
  20.8 1.1 copy.22
  22.8 5.8 %fusion.128 = bf16[512,32,64]{0,2,1:T(8,128)(2,1)S(1)} fusion(f32[512,1,64]{0,2,1:T(8,128)S(1)} %convolution_bitcast_fusion, f32[512,31,64]{0,2,1:T(8,128)} %fusion.131, bf16[1024,512]{0,1:T(8,128)(2,1)S(1)} %slice.284, bf16[8,32,8,1024]{3,2,1,0:T(8,128)(2,1)} %bitcast.237), kind=kOutput, calls=%fused_computation.199 | convolution fusion | flops 2150629376 | bytes 11534336 | tf_op jit(solution)/shard_map/cnj,jq->qnc/dot_general | solution.py:74
  28.6 6.6 %copy.28 = bf16[512,32,64]{2,1,0:T(8,128)(2,1)} copy(bf16[512,32,64]{0,2,1:T(8,128)(2,1)S(1)} %fusion.128) | data formatting | bytes 4194304 | tf_op jit(solution)/shard_map/convert_element_type | solution.py:80
  35.2 5.8 %all_to_all.38 = bf16[16,32,2048]{2,1,0:T(8,128)(2,1)S(1)} reshape(bf16[512,32,64]{2,1,0:T(8,128)(2,1)} %copy.28) | data formatting | bytes 4194304 | tf_op jit(solution)/shard_map/all_to_all | solution.py:83
  41.0 53.2 %all_to_all.51 = bf16[16,32,2048]{2,1,0:T(8,128)(2,1)S(1)} all-to-all(bf16[16,32,2048]{2,1,0:T(8,128)(2,1)S(1)} %all_to_all.38), channel_id=1, replica_groups=mesh['chan'=16,'tm'=2] {'chan'}, dimensions={0} | all-to-all | bytes 4194304 | tf_op jit(solution)/shard_map/all_to_all | solution.py:83
  94.2 1.2 copy.29
  95.3 2.4 all_to_all.41
  97.7 4.0 all-to-all-start.1
  101.8 0.7 fusion.144
  107.3 14.7 %all-gather = s32[16,64,2]{1,2,0:T(2,128)S(1)} all-gather(s32[1,64,2]{1,2,0:T(2,128)S(1)} %bitcast.252), channel_id=1, replica_groups=mesh['chan'=16,'tm'=2] {'chan'}, dimensions={0}, use_global_device_ids=true | all-gather | bytes 8704 | tf_op jit(solution)/shard_map/all_gather | solution.py:81
  122.1 6.0 %all-to-all-done.1 = bf16[2,16,32768]{2,1,0:T(8,128)(2,1)S(1)} async-done(((bf16[2,16,32768]{2,1,0:T(8,128)(2,1)}), bf16[2,16,32768]{2,1,0:T(8,128)(2,1)S(1)}, u32[]{:S(2)}, u32[]{:S(2)}) %all-to-all-start.1) | async-done | bytes 2097184 | tf_op jit(solution)/shard_map/all_to_all | solution.py:82
  128.1 5.5 %reshape.822 = bf16[8,2,2,16,32,64]{5,4,3,1,0,2:T(8,128)(2,1)} reshape(bf16[16,2,32768]{2,0,1:T(8,128)(2,1)S(1)} %bitcast.234) | data formatting | bytes 4194304 | tf_op jit(solution)/shard_map/reshape | solution.py:90
  133.6 5.3 %copy.30 = bf16[8,2,2,16,32,64]{5,4,3,2,1,0:T(8,128)(2,1)} copy(bf16[8,2,2,16,32,64]{5,4,3,1,0,2:T(8,128)(2,1)} %reshape.822) | data formatting | bytes 4194304 | tf_op jit(solution)/shard_map/while | solution.py:58
  138.9 346.0 %while.12 = (s32[]{:T(128)}, f32[4,512,8]{1,2,0:T(8,128)S(1)}, s32[]{:T(128)}, s32[4]{0:T(128)S(1)}, s32[2,2048]{1,0:T(2,128)}, /*index=5*/s32[2,1024]{1,0:T(2,1...) while((s32[]{:T(128)}, f32[4,512,8]{1,2,0:T(8,128)S(1)}, ...), condition=%wide.region_9.10_spmd, body=%wide.region_0.9_spmd.sunk | while | flops 2230321152 | bytes 46305548 | solution.py:58
  141.3 0.8 constant_dynamic-slice_fusion.2
  142.3 70.2 %cosine_convert_fusion.9 = (bf16[512,16,64]{0,2,1:T(8,128)(2,1)S(1)}, bf16[512,16,64]{0,2,1:T(8,128)(2,1)S(1)}, bf16[512,16,64]{0,2,1:T(8,128)(2,1)S(1)}, bf16[5...) fusion(s32[16,64]{1,0:T(8,128)S(1)} %mul.1666, ...), kind=kLoop, calls=%fused_computation.57.clone.1 | loop fusion | flops 47710208 | bytes 16789536 | tf_op jit(solution)/shard_map/convert
  212.5 1.5 fusion.193
  214.1 1.5 fusion.191
  215.7 1.5 fusion.189
  217.3 1.5 fusion.187
  218.9 1.5 fusion.185
  220.5 1.5 fusion.183
  222.1 1.5 fusion.181
  223.7 1.5 fusion.179
  225.4 0.6 dynamic_slice.71
  227.8 0.8 constant_dynamic-slice_fusion.2
  228.9 70.2 %cosine_convert_fusion.9 = (bf16[512,16,64]{0,2,1:T(8,128)(2,1)S(1)}, bf16[512,16,64]{0,2,1:T(8,128)(2,1)S(1)}, bf16[512,16,64]{0,2,1:T(8,128)(2,1)S(1)}, bf16[5...) fusion(s32[16,64]{1,0:T(8,128)S(1)} %mul.1666, ...), kind=kLoop, calls=%fused_computation.57.clone.1 | loop fusion | flops 47710208 | bytes 16789536 | tf_op jit(solution)/shard_map/convert
  299.0 1.5 fusion.193
  300.6 1.5 fusion.191
  302.2 1.5 fusion.189
  303.8 1.5 fusion.187
  305.4 1.5 fusion.185
  307.0 1.5 fusion.183
  308.6 1.5 fusion.181
  310.2 1.5 fusion.179
  311.9 0.6 dynamic_slice.71
  314.4 0.8 constant_dynamic-slice_fusion.2
  315.4 70.2 %cosine_convert_fusion.9 = (bf16[512,16,64]{0,2,1:T(8,128)(2,1)S(1)}, bf16[512,16,64]{0,2,1:T(8,128)(2,1)S(1)}, bf16[512,16,64]{0,2,1:T(8,128)(2,1)S(1)}, bf16[5...) fusion(s32[16,64]{1,0:T(8,128)S(1)} %mul.1666, ...), kind=kLoop, calls=%fused_computation.57.clone.1 | loop fusion | flops 47710208 | bytes 16789536 | tf_op jit(solution)/shard_map/convert
  385.5 1.5 fusion.193
  387.1 1.5 fusion.191
  388.7 1.5 fusion.189
  390.3 1.5 fusion.187
  391.9 1.5 fusion.185
  393.5 1.5 fusion.183
  395.1 1.5 fusion.181
  396.7 1.5 fusion.179
  400.9 0.8 constant_dynamic-slice_fusion.2
  401.9 70.2 %cosine_convert_fusion.9 = (bf16[512,16,64]{0,2,1:T(8,128)(2,1)S(1)}, bf16[512,16,64]{0,2,1:T(8,128)(2,1)S(1)}, bf16[512,16,64]{0,2,1:T(8,128)(2,1)S(1)}, bf16[5...) fusion(s32[16,64]{1,0:T(8,128)S(1)} %mul.1666, ...), kind=kLoop, calls=%fused_computation.57.clone.1 | loop fusion | flops 47710208 | bytes 16789536 | tf_op jit(solution)/shard_map/convert
  472.0 1.5 fusion.193
  473.6 1.5 fusion.191
  475.3 1.5 fusion.189
  476.8 1.5 fusion.187
  478.4 1.5 fusion.185
  480.0 1.5 fusion.183
  481.6 1.5 fusion.181
  483.2 1.5 fusion.179
  484.9 6.5 %all_to_all.52 = f32[2,1024,8]{1,2,0:T(8,128)S(1)} all-to-all(f32[2,1024,8]{1,2,0:T(8,128)S(1)} %bitcast.251), channel_id=1, replica_groups=mesh['chan'=16,'tm'=2] {'tm'}, dimensions={0} | all-to-all | bytes 131072 | tf_op jit(solution)/shard_map/all_to_all | solution.py:93
  491.4 0.6 copy.63
  (100 shorter events, 5.5 us)
Async XLA Ops:
  0.9 21.4 %collective-permute-start = (bf16[64,1024]{1,0:T(8,128)(2,1)S(1)}, bf16[64,1024]{1,0:T(8,128)(2,1)S(1)}, u32[]{:S(2)}, u32[]{:S(2)}) collective-permute-start(bf16[64,1024]{1,0:T(8,128)(2,1)S(1)} %slice.288), channel_id=1, source_target_pairs={{1,0},{3,2},{5,4},{7,6},{9,8},{11,10},{13,12},{15,14},{17,16},{19,... | collective-permute-start | bytes 393224 | tf_op jit(solution)/shard_map/ppermute | solution.py:14
  97.7 4.1 copy-start
  97.7 9.6 %copy-start.1 = (s32[2,64]{1,0:T(2,128)S(1)}, s32[2,64]{1,0:T(2,128)}, u32[]{:S(2)}) copy-start(s32[2,64]{1,0:T(2,128)} %param.7) | copy-start | bytes 1540
  97.7 30.4 %all-to-all-start.1 = ((bf16[2,16,32768]{2,1,0:T(8,128)(2,1)}), bf16[2,16,32768]{2,1,0:T(8,128)(2,1)S(1)}, u32[]{:S(2)}, u32[]{:S(2)}) async-start(bf16[2,16,32768]{2,1,0:T(8,128)(2,1)} %all_to_all.41), calls=%async_computation.1 | async-start | bytes 4194304 | tf_op jit(solution)/shard_map/all_to_all | solution.py:82
where the time goes:
time: 497 us; the launch traced here: 492 us
  other arithmetic  293 us (59%)
  blocking collectives  74.4 us (15%)
  matrix products  59.4 us (12%)
  local copies, waits for them, and re-layouts  41.4 us (8%)
  loops' own time  7.95 us (2%)
  waiting for transfers between devices  6 us (1%)
  starting transfers between devices  5.34 us (1%)
  between operations  4.99 us (1%)
    another operation x5, other arithmetic  291 us
    all_to_all x1, blocking collectives, shards(): lax.all_to_all(spectra, 'chan', split_axis=0, concat_axis=1, tiled=True)  53.2 us
    dot_general x32, matrix products, beam_block(): jnp.einsum('rdc,ptdnc->rptn', replica, received[local_bin], preferred_ele...  48.9 us
    all_gather x1, blocking collectives, shards(): positions = lax.all_gather(coords, 'chan', axis=1, tiled=True)  14.7 us
  transfers between devices with their start and end apart: 2, of which 1 were waited for; matrix products, arithmetic and copies ran while one was open for 4% of the time, Pallas kernels for 0%

commit v1 on v0

v1 whole, which is shorter than its diff:
```python
import functools
import math

import jax
import jax.numpy as jnp
import numpy as np
from jax import lax
from jax.experimental import pallas as pl
from jax.experimental.pallas import tpu as pltpu
from jax.sharding import PartitionSpec as P

W = 2048
REACH = 32
LANES = 128
GROUP = 8


def shifted(block, axis, distance):
    devices = range(lax.axis_size(axis))
    route = [(i - distance, i) for i in devices if i - distance in devices]
    return lax.ppermute(block, axis, route)


def taper_table(bins, width):
    offsets = jnp.arange(width, dtype=jnp.int32)
    turns = jnp.remainder(bins[None, :] * offsets[:, None], width).astype(jnp.float32) * (
        2.0 * math.pi / width
    )
    taper = 0.5 - 0.5 * jnp.cos(offsets.astype(jnp.float32) * (2.0 * math.pi / width))
    weight = (taper * math.sqrt(8.0 / (3.0 * width)))[:, None]
    table = jnp.stack([weight * jnp.cos(turns), -weight * jnp.sin(turns)], axis=-1)
    return table.reshape(width, -1).astype(jnp.bfloat16)


def circle_fit():
    u = 0.125 * (1.0 - np.cos(math.pi * (np.arange(400) + 0.5) / 400))
    t = np.sqrt(u)
    powers = u[:, None] ** np.arange(6)[None, :]
    scaled = powers * (4.0 ** np.arange(6))
    cos_fit = np.linalg.lstsq(scaled, np.cos(2 * math.pi * t), rcond=None)[0]
    sin_fit = np.linalg.lstsq(scaled, np.sin(2 * math.pi * t) / t, rcond=None)[0]
    back = 4.0 ** np.arange(6)
    return [float(v) for v in cos_fit * back], [float(v) for v in sin_fit * back]


COS_FIT, SIN_FIT = circle_fit()


def horner(u, fit):
    total = jnp.full_like(u, fit[-1])
    for value in fit[-2::-1]:
        total = total * u + value
    return total


def circle(t):
    t = t - jnp.floor(t + 0.5)
    u = t * t
    return horner(u, COS_FIT), t * horner(u, SIN_FIT)


def grid_rows(slow_index):
    first, second = slow_index[0], slow_index[1]
    low0, low1 = first < 0, second < 0
    a0, a1 = jnp.abs(first), jnp.abs(second)
    quad = jnp.where(low0 == low1, 0, 2) + low0.astype(jnp.int32)
    inner = quad * REACH * REACH + (a0 - 1) * REACH + a1 - 1
    base = 4 * REACH * REACH
    on_second = base + low1.astype(jnp.int32) * REACH + a1 - 1
    on_first = base + (2 + low0.astype(jnp.int32)) * REACH + a0 - 1
    return jnp.where(
        a0 == 0,
        jnp.where(a1 == 0, base + 4 * REACH, on_second),
        jnp.where(a1 == 0, on_first, inner),
    )


def product(rows, columns):
    return lax.dot_general(
        rows, columns, (((1,), (1,)), ((), ())), preferred_element_type=jnp.float32
    )


def beam_kernel(
    scale, bins_ref, pick_ref, pos_ref, recv_ref, out_ref,
    xt, xj, c0, s0, c1, s1, ra, rb, grid_power,
):
    slots, tm_count, chan_count, tiles, _ = recv_ref.shape
    per_dev = slots // 2
    half = LANES // 2
    side = tm_count * 2 * tiles
    modulus = 5 * W // 2
    lane = lax.broadcasted_iota(jnp.int32, (1, LANES), 1)
    steps = (lax.broadcasted_iota(jnp.int32, (REACH, 1), 0) + 1).astype(jnp.float32)

    def one_bin(f, _):
        bin_value = bins_ref[f].astype(jnp.float32)
        for axis, cos_ref, sin_ref in ((0, c0, s0), (1, c1, s1)):
            turn = pos_ref[axis : axis + 1, :].astype(jnp.float32) * bin_value
            turn = (turn - modulus * jnp.floor(turn * (1.0 / modulus))) * (1.0 / modulus)
            turn = turn - jnp.floor(turn + 0.5)
            cosine, sine = circle(turn * steps)
            cos_ref[...] = cosine
            sin_ref[...] = sine
        for p in range(2):
            for t in range(tm_count):
                for m in range(chan_count // 2):
                    left = recv_ref[2 * f + p, t, 2 * m].astype(jnp.float32)
                    right = recv_ref[2 * f + p, t, 2 * m + 1].astype(jnp.float32)
                    even = jnp.where(lane < half, left, pltpu.roll(right, half, 1))
                    odd = jnp.where(lane < half, pltpu.roll(left, half, 1), right)
                    for parity, value in enumerate((even, odd)):
                        row = (t * 2 + parity) * tiles
                        cols = slice(m * LANES, (m + 1) * LANES)
                        xt[p * side + row : p * side + row + tiles, cols] = value.astype(xt.dtype)
                        q = 1 - p
                        value = value if p else -value
                        xj[q * side + row : q * side + row + tiles, cols] = value.astype(xj.dtype)

        def put(row, values):
            total = jnp.sum(values * values, axis=1, keepdims=True)
            rows = pl.ds(row, values.shape[0])
            grid_power[rows, :] = jnp.where(lane == f, total, grid_power[rows, :])

        def one_group(g, _):
            for k in range(GROUP):
                cos_row = c0[pl.ds(g * GROUP + k, 1), :]
                sin_row = s0[pl.ds(g * GROUP + k, 1), :]
                cosines, sines = c1[...], s1[...]
                at = 2 * REACH * k
                ra[at : at + REACH, :] = (cos_row * cosines).astype(ra.dtype)
                ra[at + REACH : at + 2 * REACH, :] = (sin_row * sines).astype(ra.dtype)
                rb[at : at + REACH, :] = (sin_row * cosines).astype(rb.dtype)
                rb[at + REACH : at + 2 * REACH, :] = (cos_row * sines).astype(rb.dtype)
            da = product(ra[...], xt[...])
            db = product(rb[...], xj[...])
            for k in range(GROUP):
                at = 2 * REACH * k
                cc, ss = da[at : at + REACH], da[at + REACH : at + 2 * REACH]
                sc, cs = db[at : at + REACH], db[at + REACH : at + 2 * REACH]
                even_same, even_other = cc - ss, cc + ss
                odd_same, odd_other = sc + cs, sc - cs
                row = pl.multiple_of((g * GROUP + k) * REACH, REACH)
                put(row, even_same + odd_same)
                put(row + REACH * REACH, even_same - odd_same)
                put(row + 2 * REACH * REACH, even_other + odd_other)
                put(row + 3 * REACH * REACH, even_other - odd_other)
            return 0

        lax.fori_loop(0, REACH // GROUP, one_group, 0)
        ra[0:REACH, :] = c1[...].astype(ra.dtype)
        ra[REACH : 2 * REACH, :] = c0[...].astype(ra.dtype)
        ra[2 * REACH : 2 * REACH + 16, :] = jnp.ones((16, ra.shape[1]), ra.dtype)
        rb[0:REACH, :] = s1[...].astype(rb.dtype)
        rb[REACH : 2 * REACH, :] = s0[...].astype(rb.dtype)
        da = product(ra[0 : 2 * REACH + 16, :], xt[...])
        db = product(rb[0 : 2 * REACH, :], xj[...])
        base = 4 * REACH * REACH
        for k in range(2):
            rows = slice(k * REACH, (k + 1) * REACH)
            put(base + 2 * k * REACH, da[rows] + db[rows])
            put(base + (2 * k + 1) * REACH, da[rows] - db[rows])
        put(base + 4 * REACH, da[2 * REACH :])
        return 0

    lax.fori_loop(0, per_dev, one_bin, 0)

    def pick(block, _):
        start = pl.multiple_of(block * 8, 8)
        for k in range(8):
            out_ref[pl.ds(start + k, 1), :] = grid_power[pl.ds(pick_ref[start + k], 1), :] * scale
        return 0

    lax.fori_loop(0, out_ref.shape[0] // 8, pick, 0)


def beam(received, my_bins, positions, slow_index, scale):
    _, tm_count, chan_count, tiles, _ = received.shape
    channels = positions.shape[1]
    columns = 4 * tm_count * tiles
    half_rows = 2 * REACH * GROUP
    vmem = pl.BlockSpec(memory_space=pltpu.VMEM)
    smem = pl.BlockSpec(memory_space=pltpu.SMEM)
    table = pltpu.VMEM((REACH, channels), jnp.float32)
    return pl.pallas_call(
        functools.partial(beam_kernel, scale),
        out_shape=jax.ShapeDtypeStruct((slow_index.shape[1], LANES), jnp.float32),
        in_specs=[smem, smem, vmem, vmem],
        out_specs=vmem,
        scratch_shapes=[
            pltpu.VMEM((columns, channels), jnp.bfloat16),
            pltpu.VMEM((columns, channels), jnp.bfloat16),
            table, table, table, table,
            pltpu.VMEM((half_rows, channels), jnp.bfloat16),
            pltpu.VMEM((half_rows, channels), jnp.bfloat16),
            pltpu.VMEM((4 * REACH * REACH + 4 * REACH + 16, LANES), jnp.float32),
        ],
        compiler_params=pltpu.CompilerParams(vmem_limit_bytes=48 * 2**20),
        cost_estimate=pl.CostEstimate(
            flops=16 * REACH * REACH * columns * channels * my_bins.shape[0],
            bytes_accessed=received.size * 2,
            transcendentals=0,
        ),
    )(my_bins, grid_rows(slow_index), positions, received)


def shards(records, coords, bins, slow_index):
    ch_dev, local_samples = records.shape
    hop = W // 2
    snaps_dev = local_samples // hop
    chan_count = lax.axis_size("chan")
    tm_count = lax.axis_size("tm")
    channels = ch_dev * chan_count
    freq = bins.shape[0]
    scale = 1.0 / (channels * snaps_dev * tm_count)
    table = taper_table(bins, W)
    blocks = records.reshape(ch_dev, snaps_dev, hop)
    following = shifted(records[:, :hop], "tm", -1)
    first = jnp.einsum("cnj,jq->qnc", blocks, table[:hop], preferred_element_type=jnp.float32)
    second = jnp.einsum(
        "cnj,jq->qnc", blocks[:, 1:], table[hop:], preferred_element_type=jnp.float32
    )
    tail = jnp.einsum("cj,jq->qc", following, table[hop:], preferred_element_type=jnp.float32)
    second = jnp.concatenate([second, tail[:, None, :]], axis=1)
    spectra = (first + second).astype(jnp.bfloat16).reshape(2 * freq, snaps_dev * ch_dev)
    positions = lax.all_gather(coords, "chan", axis=1, tiled=True)
    received = lax.all_to_all(
        lax.all_to_all(spectra, "chan", split_axis=0, concat_axis=1, tiled=True),
        "tm",
        split_axis=0,
        concat_axis=1,
        tiled=True,
    )
    per_dev = freq // (chan_count * tm_count)
    tiles = snaps_dev * ch_dev // LANES
    received = received.reshape(2 * per_dev, tm_count, chan_count, tiles, LANES)
    bin_base = (lax.axis_index("chan") * tm_count + lax.axis_index("tm")) * per_dev
    my_bins = lax.dynamic_slice_in_dim(bins, bin_base, per_dev, 0)
    whole = beam(received, my_bins, positions, slow_index, scale)[:, :per_dev]
    return lax.all_to_all(whole, "tm", split_axis=0, concat_axis=1, tiled=True)


def solution(mesh):
    return jax.shard_map(
        shards,
        mesh=mesh,
        in_specs=(P("chan", "tm"), P(None, "chan"), P(), P()),
        out_specs=P("tm", "chan"),
        check_vma=False,
    )
```

time: 497 us -> 175 us (0.35)
  other arithmetic: 293 us -> 10.1 us
  matrix products: 59.4 us -> 10.5 us
  Pallas kernels: 0 us -> 36 us
  local copies, waits for them, and re-layouts: 41.4 us -> 24.7 us
  loops' own time: 7.95 us -> 0 us
  waiting for transfers between devices: 6 us -> 11.4 us
    another operation x5 -> x1, other arithmetic: 291 us -> 9.87 us
    dot_general x32 -> x0, matrix products: 48.9 us -> none  [beam_block(): jnp.einsum('rdc,ptdnc->rptn', replica, received[local_bin], preferred_ele...]
    pallas_call x0 -> x1, Pallas kernels: none -> 36 us  [beam(): pl.pallas_call(functools.partial(beam_kernel, scale), out_shape=jax.Shape...]
    another operation x1 -> x0, loops' own time: 7.95 us -> none  [beam_rows(): return lax.map(beam_block, starts).reshape(count, bin_count)]
    all_to_all x1, waiting for transfers between devices: 6 us -> 11.4 us  [shards(): lax.all_to_all(lax.all_to_all(spectra, 'chan', split_axis=0, concat_axis=...]
    while x1 -> x0, local copies, waits for them, and re-layouts: 5.29 us -> none  [beam_rows(): return lax.map(beam_block, starts).reshape(count, bin_count)]
  transfers between devices with their start and end apart: 2 -> 2, of which waited for: 1 -> 1; matrix products, arithmetic and copies ran while one was open for 4% -> 12% of each run, Pallas kernels for 0% -> 0%
where the time goes in v1:
time: 175 us; the launch traced here: 173 us
  blocking collectives  74.3 us (42%)
  Pallas kernels  36 us (21%)
  local copies, waits for them, and re-layouts  24.7 us (14%)
  waiting for transfers between devices  11.4 us (7%)
  matrix products  10.5 us (6%)
  other arithmetic  10.1 us (6%)
  starting transfers between devices  5.33 us (3%)
    all_to_all x1, blocking collectives, shards(): lax.all_to_all(spectra, 'chan', split_axis=0, concat_axis=1, tiled=True)  53.2 us
    pallas_call x1, Pallas kernels, beam(): pl.pallas_call(functools.partial(beam_kernel, scale), out_shape=jax.Shape...  36 us
    all_gather x1, blocking collectives, shards(): positions = lax.all_gather(coords, 'chan', axis=1, tiled=True)  14.6 us
    all_to_all x1, waiting for transfers between devices, shards(): lax.all_to_all(lax.all_to_all(spectra, 'chan', split_axis=0, concat_axis=...  11.4 us
    another operation x1, other arithmetic  9.87 us
    all_to_all x2, local copies, waits for them, and re-layouts, shards(): lax.all_to_all(spectra, 'chan', split_axis=0, concat_axis=1, tiled=True)  6.91 us
    convert_element_type x1, local copies, waits for them, and re-layouts, shards(): (first + second).astype(jnp.bfloat16).reshape(2 * freq, snaps_dev * ch_dev)  6.64 us
    all_to_all x1, blocking collectives, shards(): return lax.all_to_all(whole, 'tm', split_axis=0, concat_axis=1, tiled=True)  6.5 us
  transfers between devices with their start and end apart: 2, of which 1 were waited for; matrix products, arithmetic and copies ran while one was open for 12% of the time, Pallas kernels for 0%

profile of v1, /device:TPU:10, one launch (start us, length us, event | category | flops | bytes accessed | tf_op | source)
XLA Modules:
  0.0 172.5 jit_solution(4401629434076465720)
XLA Ops:
  0.0 0.9 slice.35
  0.9 1.3 collective-permute-start
  2.2 0.1 subtract_multiply_fusion
  2.3 9.9 %multiply_convert_fusion.1 = (bf16[2048,256,1]{1,0,2:T(8,128)(2,1)S(1)}, bf16[2048,256,1]{1,0,2:T(8,128)(2,1)S(1)}) fusion(s32[256]{0:T(256)} %param.6, f32[2048]{0:T(1024)S(1)} %get-tuple-element.9, f32[2048]{0:T(1024)S(1)} %get-tuple-element.10), kind=kLoop, calls=%fused_computation.15 | loop fusion | flops 9437184 | bytes 2114560 | tf_op jit(solution)/shard_map/convert
  12.2 0.1 fusion.12
  12.3 1.1 copy.29
  13.4 0.4 slice.33
  13.9 2.6 %copy.45 = bf16[8,32,8,1024]{3,2,0,1:T(8,128)(2,1)S(1)} copy(bf16[8,32,8,1024]{3,2,1,0:T(8,128)(2,1)} %bitcast.49) | data formatting | bytes 8388608 | tf_op jit(solution)/shard_map/reshape | solution.py:217
  16.5 4.2 %fusion.3 = f32[512,31,64]{0,2,1:T(8,128)} fusion(bf16[64,32,1024]{2,0,1:T(8,128)(2,1)S(1)} %bitcast.51, bf16[1024,512]{0,1:T(8,128)(2,1)S(1)} %slice.33), kind=kOutput, calls=%fused_computation.8 | convolution fusion | flops 2080374784 | bytes 9175040 | tf_op jit(solution)/shard_map/cnj,jq->qnc/dot_general | solution.py:220
  20.7 1.1 copy.26
  21.8 0.4 slice.31
  22.3 0.0 collective-permute-done
  22.3 0.4 convolution_bitcast_fusion
  22.8 5.8 %fusion = bf16[512,32,64]{0,2,1:T(8,128)(2,1)S(1)} fusion(f32[512,1,64]{0,2,1:T(8,128)S(1)} %convolution_bitcast_fusion, f32[512,31,64]{0,2,1:T(8,128)} %fusion.3, bf16[1024,512]{0,1:T(8,128)(2,1)S(1)} %slice.31, bf16[8,32,8,1024]{3,2,1,0:T(8,128)(2,1)} %bitcast.50), kind=kOutput, calls=%fused_computation.2 | convolution fusion | flops 2150629376 | bytes 11534336 | tf_op jit(solution)/shard_map/cnj,jq->qnc/dot_general | solution.py:219
  28.6 6.6 %copy.32 = bf16[512,32,64]{2,1,0:T(8,128)(2,1)} copy(bf16[512,32,64]{0,2,1:T(8,128)(2,1)S(1)} %fusion) | data formatting | bytes 4194304 | tf_op jit(solution)/shard_map/convert_element_type | solution.py:225
  35.2 5.8 %all_to_all.38 = bf16[16,32,2048]{2,1,0:T(8,128)(2,1)S(1)} reshape(bf16[512,32,64]{2,1,0:T(8,128)(2,1)} %copy.32) | data formatting | bytes 4194304 | tf_op jit(solution)/shard_map/all_to_all | solution.py:228
  41.0 53.2 %all_to_all.51 = bf16[16,32,2048]{2,1,0:T(8,128)(2,1)S(1)} all-to-all(bf16[16,32,2048]{2,1,0:T(8,128)(2,1)S(1)} %all_to_all.38), channel_id=1, replica_groups=mesh['chan'=16,'tm'=2] {'chan'}, dimensions={0} | all-to-all | bytes 4194304 | tf_op jit(solution)/shard_map/all_to_all | solution.py:228
  94.2 1.2 copy.33
  95.3 2.4 %all_to_all.41 = bf16[2,16,32768]{2,1,0:T(8,128)(2,1)} reshape(bf16[32,16,2048]{2,1,0:T(8,128)(2,1)S(1)} %copy.33) | data formatting | bytes 4194304 | tf_op jit(solution)/shard_map/all_to_all | solution.py:227
  97.7 0.0 copy-start.1
  97.7 0.0 copy-start.2
  97.7 0.0 copy-start
  97.7 4.0 %all-to-all-start.1 = ((bf16[2,16,32768]{2,1,0:T(8,128)(2,1)}), bf16[2,16,32768]{2,1,0:T(8,128)(2,1)S(1)}, u32[]{:S(2)}, u32[]{:S(2)}) async-start(bf16[2,16,32768]{2,1,0:T(8,128)(2,1)} %all_to_all.41), calls=%async_computation.1 | async-start | bytes 4194304 | tf_op jit(solution)/shard_map/all_to_all | solution.py:227
  101.7 0.0 copy-done.1
  101.7 0.1 dynamic_slice.3.bins_ref
  101.8 0.0 copy-done.2
  101.8 14.6 %all-gather = s32[16,64,2]{1,2,0:T(2,128)S(1)} all-gather(s32[1,64,2]{1,2,0:T(2,128)S(1)} %bitcast.53), channel_id=1, replica_groups=mesh['chan'=16,'tm'=2] {'chan'}, dimensions={0}, use_global_device_ids=true | all-gather | bytes 8704 | tf_op jit(solution)/shard_map/all_gather | solution.py:226
  116.5 0.1 reshape.226
  116.5 0.0 copy-done
  116.5 0.1 compare_select_fusion
  116.6 11.4 %all-to-all-done.1 = bf16[2,16,32768]{2,1,0:T(8,128)(2,1)S(1)} async-done(((bf16[2,16,32768]{2,1,0:T(8,128)(2,1)}), bf16[2,16,32768]{2,1,0:T(8,128)(2,1)S(1)}, u32[]{:S(2)}, u32[]{:S(2)}) %all-to-all-start.1) | async-done | bytes 2097184 | tf_op jit(solution)/shard_map/all_to_all | solution.py:227
  128.1 0.5 copy.42
  128.5 0.6 copy.40.recv_ref
  129.1 36.0 %shard_map.46 = f32[2048,128]{1,0:T(8,128)S(1)} custom-call(s32[8]{0:T(128)S(1)} %dynamic_slice.3.bins_ref, s32[2048]{0:T(1024)S(1)} %bitcast.45, s32[2,1024]{1,0:T(2,128)S(1)} %bitcast.44, bf16[16,2,16,16,128]{4,3,2,1,0:T(8,128)(2,1)S(1)} %copy.40.recv_ref), custom_call_target="tpu_custom_call" | custom-call | flops 17179869184 | bytes 2097152 | tf_op jit(solution)/shard_map/pallas_call | solution.py:185
  165.1 0.3 copy.35
  165.4 6.5 %all_to_all.52 = f32[2,1024,8]{1,2,0:T(8,128)S(1)} all-to-all(f32[2,1024,8]{1,2,0:T(8,128)S(1)} %copy.35), channel_id=1, replica_groups=mesh['chan'=16,'tm'=2] {'tm'}, dimensions={0} | all-to-all | bytes 131072 | tf_op jit(solution)/shard_map/all_to_all | solution.py:240
  171.9 0.6 copy.47
  (1 shorter events, 0.0 us)
Async XLA Ops:
  0.9 21.4 %collective-permute-start = (bf16[64,1024]{1,0:T(8,128)(2,1)S(1)}, bf16[64,1024]{1,0:T(8,128)(2,1)S(1)}, u32[]{:S(2)}, u32[]{:S(2)}) collective-permute-start(bf16[64,1024]{1,0:T(8,128)(2,1)S(1)} %slice.35), channel_id=1, source_target_pairs={{1,0},{3,2},{5,4},{7,6},{9,8},{11,10},{13,12},{15,14},{17,16},{19,... | collective-permute-start | bytes 393224 | tf_op jit(solution)/shard_map/ppermute | solution.py:21
  97.7 4.0 %copy-start.1 = (s32[256]{0:T(256)S(1)}, s32[256]{0:T(256)}, u32[]{:S(2)}) copy-start(s32[256]{0:T(256)} %param.6) | copy-start | bytes 3076
  97.7 4.1 %copy-start.2 = (s32[2,64]{1,0:T(2,128)S(1)}, s32[2,64]{1,0:T(2,128)}, u32[]{:S(2)}) copy-start(s32[2,64]{1,0:T(2,128)} %param.5) | copy-start | bytes 1540
  97.7 18.9 %copy-start = (s32[2,2048]{1,0:T(2,128)S(1)}, s32[2,2048]{1,0:T(2,128)}, u32[]{:S(2)}) copy-start(s32[2,2048]{1,0:T(2,128)} %param.7) | copy-start | bytes 49156
  97.7 30.4 %all-to-all-start.1 = ((bf16[2,16,32768]{2,1,0:T(8,128)(2,1)}), bf16[2,16,32768]{2,1,0:T(8,128)(2,1)S(1)}, u32[]{:S(2)}, u32[]{:S(2)}) async-start(bf16[2,16,32768]{2,1,0:T(8,128)(2,1)} %all_to_all.41), calls=%async_computation.1 | async-start | bytes 4194304 | tf_op jit(solution)/shard_map/all_to_all | solution.py:227

commit v2 on v1

--- a/solution.py
+++ b/solution.py
@@ -13,23 +13,7 @@
 REACH = 32
 LANES = 128
 GROUP = 8
-
-
-def shifted(block, axis, distance):
-    devices = range(lax.axis_size(axis))
-    route = [(i - distance, i) for i in devices if i - distance in devices]
-    return lax.ppermute(block, axis, route)
-
-
-def taper_table(bins, width):
-    offsets = jnp.arange(width, dtype=jnp.int32)
-    turns = jnp.remainder(bins[None, :] * offsets[:, None], width).astype(jnp.float32) * (
-        2.0 * math.pi / width
-    )
-    taper = 0.5 - 0.5 * jnp.cos(offsets.astype(jnp.float32) * (2.0 * math.pi / width))
-    weight = (taper * math.sqrt(8.0 / (3.0 * width)))[:, None]
-    table = jnp.stack([weight * jnp.cos(turns), -weight * jnp.sin(turns)], axis=-1)
-    return table.reshape(width, -1).astype(jnp.bfloat16)
+CHUNKS = 4
 
 
 def circle_fit():
@@ -81,32 +65,175 @@
     )
 
 
-def beam_kernel(
-    scale, bins_ref, pick_ref, pos_ref, recv_ref, out_ref,
+def kernel(
+    scale, tm_count, chan_count, bins_ref, pick_ref, bin_rows, coords_ref, records_ref, out_ref,
+    blocks, table, stage, send, recv, digits, all_digits, positions,
     xt, xj, c0, s0, c1, s1, ra, rb, grid_power,
+    load_sem, halo_sems, digit_sems, send_sem, recv_sems,
 ):
-    slots, tm_count, chan_count, tiles, _ = recv_ref.shape
-    per_dev = slots // 2
+    devices = tm_count * chan_count
+    chunks, _, chunk_rows, _ = recv.shape
+    ch_dev, local_samples = records_ref.shape
+    hop = W // 2
+    snaps = local_samples // hop
+    tiles = snaps * ch_dev // LANES
+    freq_rows = bin_rows.shape[0]
+    per_dev = bins_ref.shape[0]
+    per_chunk = per_dev // chunks
     half = LANES // 2
     side = tm_count * 2 * tiles
+    my_chan, my_tm = lax.axis_index("chan"), lax.axis_index("tm")
+    me = my_chan * tm_count + my_tm
+    lane = lax.broadcasted_iota(jnp.int32, (1, LANES), 1)
+    mesh_id = pl.DeviceIdType.MESH
+
+    barrier = pltpu.get_barrier_semaphore()
+
+    def greet(j, _):
+        other = lax.rem(me + j, devices)
+        pl.semaphore_signal(
+            barrier,
+            inc=1,
+            device_id=(lax.div(other, tm_count), lax.rem(other, tm_count)),
+            device_id_type=mesh_id,
+        )
+        return 0
+
+    lax.fori_loop(1, devices, greet, 0)
+
+    def load(n, _):
+        pltpu.make_async_copy(
+            records_ref.at[:, pl.ds(pl.multiple_of(n * hop, hop), hop)],
+            blocks.at[pl.ds(pl.multiple_of(n * ch_dev, ch_dev), ch_dev), :],
+            load_sem,
+        ).start()
+        return 0
+
+    lax.fori_loop(0, snaps, load, 0)
+    digits[...] = jnp.zeros_like(digits)
+    for axis in range(2):
+        values = coords_ref[axis : axis + 1, :].astype(jnp.float32)
+        high = jnp.floor(values * (1.0 / 32.0))
+        digits[2 * axis : 2 * axis + 1, :] = high.astype(digits.dtype)
+        digits[2 * axis + 1 : 2 * axis + 2, :] = (values - 32.0 * high).astype(digits.dtype)
+    all_digits[my_chan] = digits[...]
+    pl.semaphore_wait(barrier, devices - 1)
+
+    halo = pltpu.make_async_remote_copy(
+        src_ref=records_ref.at[:, 0:hop],
+        dst_ref=blocks.at[snaps * ch_dev : (snaps + 1) * ch_dev, :],
+        send_sem=halo_sems.at[0],
+        recv_sem=halo_sems.at[1],
+        device_id=(my_chan, lax.rem(my_tm + tm_count - 1, tm_count)),
+        device_id_type=mesh_id,
+    )
+    halo.start()
+
+    def tell(j, _):
+        pltpu.make_async_remote_copy(
+            src_ref=digits,
+            dst_ref=all_digits.at[my_chan],
+            send_sem=digit_sems.at[0],
+            recv_sem=digit_sems.at[1],
+            device_id=(lax.rem(my_chan + j, chan_count), my_tm),
+            device_id_type=mesh_id,
+        ).start()
+        return 0
+
+    lax.fori_loop(1, chan_count, tell, 0)
+
+    offset = lax.broadcasted_iota(jnp.int32, (1, W), 1).astype(jnp.float32) * (1.0 / W)
+    weight = (0.5 - 0.5 * circle(offset)[0]) * math.sqrt(8.0 / (3.0 * W))
+    quarter = lax.rem(lax.broadcasted_iota(jnp.int32, (16, 1), 0), 2).astype(jnp.float32) * 0.25
+
+    def table_rows(r, _):
+        rows = pl.ds(pl.multiple_of(r * 16, 16), 16)
+        turn = bin_rows[rows, :].astype(jnp.float32) * offset + quarter
+        turn = turn - jnp.floor(turn + 0.5)
+        table[rows, :] = (weight * horner(turn * turn, COS_FIT)).astype(table.dtype)
+        return 0
+
+    lax.fori_loop(0, freq_rows // 16, table_rows, 0)
+
+    whole = blocks.at[0 : snaps * ch_dev, :]
+    pltpu.make_async_copy(whole, whole, load_sem).wait()
+    halo.wait()
+    tail = blocks[snaps * ch_dev :, :]
+    blocks[snaps * ch_dev :, :] = jnp.where(my_tm == tm_count - 1, jnp.zeros_like(tail), tail)
+
+    def transform(i, _):
+        start = pl.multiple_of(i * 2 * LANES, 2 * LANES)
+        here = blocks[pl.ds(start, 2 * LANES), :]
+        after = blocks[pl.ds(start + ch_dev, 2 * LANES), :]
+        out = product(table[:, :hop], here) + product(table[:, hop:], after)
+        for k in range(2):
+            rows = pl.ds(2 * i + k, freq_rows, stride=tiles)
+            stage[rows, :] = out[:, k * LANES : (k + 1) * LANES]
+        return 0
+
+    lax.fori_loop(0, tiles // 2, transform, 0)
+    dest_rows = chunks * chunk_rows
+
+    def pack(d, _):
+        rows = pl.ds(pl.multiple_of(d * dest_rows, dest_rows), dest_rows)
+        send[rows, :] = stage[rows, :].astype(send.dtype)
+        return 0
+
+    lax.fori_loop(0, devices, pack, 0)
+
+    def part(k, d):
+        start = d * dest_rows + k * chunk_rows
+        return pl.ds(pl.multiple_of(start, chunk_rows), chunk_rows)
+
+    def send_chunk(k, _):
+        def send_one(j, _):
+            other = lax.rem(me + j, devices)
+            pltpu.make_async_remote_copy(
+                src_ref=send.at[part(k, other), :],
+                dst_ref=recv.at[k, me],
+                send_sem=send_sem,
+                recv_sem=recv_sems.at[k],
+                device_id=(lax.div(other, tm_count), lax.rem(other, tm_count)),
+                device_id_type=mesh_id,
+            ).start()
+            return 0
+
+        lax.fori_loop(1, devices, send_one, 0)
+        recv[k, me] = send[part(k, me), :]
+        return 0
+
+    lax.fori_loop(0, chunks, send_chunk, 0)
+
+    others = all_digits.at[0 : chan_count - 1]
+    pltpu.make_async_copy(others, others, digit_sems.at[1]).wait()
+    pltpu.make_async_copy(others, others, digit_sems.at[0]).wait()
+    for m in range(chan_count // 2):
+        left = all_digits[2 * m].astype(jnp.float32)
+        right = all_digits[2 * m + 1].astype(jnp.float32)
+        both = jnp.where(lane < half, left, right)
+        for axis in range(2):
+            high, low = both[2 * axis : 2 * axis + 1], both[2 * axis + 1 : 2 * axis + 2]
+            positions[axis : axis + 1, m * LANES : (m + 1) * LANES] = 32.0 * high + low
+
     modulus = 5 * W // 2
-    lane = lax.broadcasted_iota(jnp.int32, (1, LANES), 1)
     steps = (lax.broadcasted_iota(jnp.int32, (REACH, 1), 0) + 1).astype(jnp.float32)
 
-    def one_bin(f, _):
+    def one_bin(k, local, _):
+        f = k * per_chunk + local
         bin_value = bins_ref[f].astype(jnp.float32)
         for axis, cos_ref, sin_ref in ((0, c0, s0), (1, c1, s1)):
-            turn = pos_ref[axis : axis + 1, :].astype(jnp.float32) * bin_value
+            turn = positions[axis : axis + 1, :] * bin_value
             turn = (turn - modulus * jnp.floor(turn * (1.0 / modulus))) * (1.0 / modulus)
             turn = turn - jnp.floor(turn + 0.5)
             cosine, sine = circle(turn * steps)
             cos_ref[...] = cosine
             sin_ref[...] = sine
         for p in range(2):
+            source_rows = pl.ds(pl.multiple_of((2 * local + p) * tiles, tiles), tiles)
             for t in range(tm_count):
                 for m in range(chan_count // 2):
-                    left = recv_ref[2 * f + p, t, 2 * m].astype(jnp.float32)
-                    right = recv_ref[2 * f + p, t, 2 * m + 1].astype(jnp.float32)
+                    left = recv[k, 2 * m * tm_count + t, source_rows, :].astype(jnp.float32)
+                    right = recv[k, (2 * m + 1) * tm_count + t, source_rows, :].astype(jnp.float32)
                     even = jnp.where(lane < half, left, pltpu.roll(right, half, 1))
                     odd = jnp.where(lane < half, pltpu.roll(left, half, 1), right)
                     for parity, value in enumerate((even, odd)):
@@ -163,7 +290,15 @@
         put(base + 4 * REACH, da[2 * REACH :])
         return 0
 
-    lax.fori_loop(0, per_dev, one_bin, 0)
+    grid_power[...] = jnp.zeros_like(grid_power)
+
+    def one_chunk(k, _):
+        arrived = recv.at[k, 0 : devices - 1]
+        pltpu.make_async_copy(arrived, arrived, recv_sems.at[k]).wait()
+        lax.fori_loop(0, per_chunk, functools.partial(one_bin, k), 0)
+        return 0
+
+    lax.fori_loop(0, chunks, one_chunk, 0)
 
     def pick(block, _):
         start = pl.multiple_of(block * 8, 8)
@@ -172,72 +307,69 @@
         return 0
 
     lax.fori_loop(0, out_ref.shape[0] // 8, pick, 0)
-
-
-def beam(received, my_bins, positions, slow_index, scale):
-    _, tm_count, chan_count, tiles, _ = received.shape
-    channels = positions.shape[1]
+    sent = send.at[0 : (devices - 1) * dest_rows, :]
+    pltpu.make_async_copy(sent, sent, send_sem).wait()
+
+
+def shards(records, coords, bins, slow_index):
+    ch_dev, local_samples = records.shape
+    hop = W // 2
+    snaps = local_samples // hop
+    chan_count = lax.axis_size("chan")
+    tm_count = lax.axis_size("tm")
+    devices = chan_count * tm_count
+    channels = ch_dev * chan_count
+    freq = bins.shape[0]
+    per_dev = freq // devices
+    chunks = math.gcd(per_dev, CHUNKS)
+    tiles = snaps * ch_dev // LANES
+    chunk_rows = 2 * per_dev * tiles // chunks
     columns = 4 * tm_count * tiles
     half_rows = 2 * REACH * GROUP
+    scale = 1.0 / (channels * snaps * tm_count)
+    bin_base = (lax.axis_index("chan") * tm_count + lax.axis_index("tm")) * per_dev
+    my_bins = lax.dynamic_slice_in_dim(bins, bin_base, per_dev, 0)
+    bin_rows = jnp.repeat(bins, 2)[:, None]
+    twice = jnp.concatenate([coords] * (LANES // ch_dev), axis=1)
     vmem = pl.BlockSpec(memory_space=pltpu.VMEM)
     smem = pl.BlockSpec(memory_space=pltpu.SMEM)
-    table = pltpu.VMEM((REACH, channels), jnp.float32)
-    return pl.pallas_call(
-        functools.partial(beam_kernel, scale),
+    angles = pltpu.VMEM((REACH, channels), jnp.float32)
+    picked = pl.pallas_call(
+        functools.partial(kernel, scale, tm_count, chan_count),
         out_shape=jax.ShapeDtypeStruct((slow_index.shape[1], LANES), jnp.float32),
-        in_specs=[smem, smem, vmem, vmem],
+        in_specs=[smem, smem, vmem, vmem, pl.BlockSpec(memory_space=pl.ANY)],
         out_specs=vmem,
         scratch_shapes=[
+            pltpu.VMEM(((snaps + 1) * ch_dev, hop), jnp.bfloat16),
+            pltpu.VMEM((2 * freq, W), jnp.bfloat16),
+            pltpu.VMEM((2 * freq * tiles, LANES), jnp.float32),
+            pltpu.VMEM((2 * freq * tiles, LANES), jnp.bfloat16),
+            pltpu.VMEM((chunks, devices, chunk_rows, LANES), jnp.bfloat16),
+            pltpu.VMEM((16, LANES), jnp.bfloat16),
+            pltpu.VMEM((chan_count, 16, LANES), jnp.bfloat16),
+            pltpu.VMEM((2, channels), jnp.float32),
             pltpu.VMEM((columns, channels), jnp.bfloat16),
             pltpu.VMEM((columns, channels), jnp.bfloat16),
-            table, table, table, table,
+            angles, angles, angles, angles,
             pltpu.VMEM((half_rows, channels), jnp.bfloat16),
             pltpu.VMEM((half_rows, channels), jnp.bfloat16),
             pltpu.VMEM((4 * REACH * REACH + 4 * REACH + 16, LANES), jnp.float32),
+            pltpu.SemaphoreType.DMA,
+            pltpu.SemaphoreType.DMA((2,)),
+            pltpu.SemaphoreType.DMA((2,)),
+            pltpu.SemaphoreType.DMA,
+            pltpu.SemaphoreType.DMA((chunks,)),
         ],
-        compiler_params=pltpu.CompilerParams(vmem_limit_bytes=48 * 2**20),
+        compiler_params=pltpu.CompilerParams(
+            collective_id=0, has_side_effects=True, vmem_limit_bytes=52 * 2**20
+        ),
         cost_estimate=pl.CostEstimate(
-            flops=16 * REACH * REACH * columns * channels * my_bins.shape[0],
-            bytes_accessed=received.size * 2,
+            flops=16 * REACH * REACH * columns * channels * per_dev,
+            bytes_accessed=records.size * 2,
             transcendentals=0,
         ),
-    )(my_bins, grid_rows(slow_index), positions, received)
-
-
-def shards(records, coords, bins, slow_index):
-    ch_dev, local_samples = records.shape
-    hop = W // 2
-    snaps_dev = local_samples // hop
-    chan_count = lax.axis_size("chan")
-    tm_count = lax.axis_size("tm")
-    channels = ch_dev * chan_count
-    freq = bins.shape[0]
-    scale = 1.0 / (channels * snaps_dev * tm_count)
-    table = taper_table(bins, W)
-    blocks = records.reshape(ch_dev, snaps_dev, hop)
-    following = shifted(records[:, :hop], "tm", -1)
-    first = jnp.einsum("cnj,jq->qnc", blocks, table[:hop], preferred_element_type=jnp.float32)
-    second = jnp.einsum(
-        "cnj,jq->qnc", blocks[:, 1:], table[hop:], preferred_element_type=jnp.float32
-    )
-    tail = jnp.einsum("cj,jq->qc", following, table[hop:], preferred_element_type=jnp.float32)
-    second = jnp.concatenate([second, tail[:, None, :]], axis=1)
-    spectra = (first + second).astype(jnp.bfloat16).reshape(2 * freq, snaps_dev * ch_dev)
-    positions = lax.all_gather(coords, "chan", axis=1, tiled=True)
-    received = lax.all_to_all(
-        lax.all_to_all(spectra, "chan", split_axis=0, concat_axis=1, tiled=True),
-        "tm",
-        split_axis=0,
-        concat_axis=1,
-        tiled=True,
-    )
-    per_dev = freq // (chan_count * tm_count)
-    tiles = snaps_dev * ch_dev // LANES
-    received = received.reshape(2 * per_dev, tm_count, chan_count, tiles, LANES)
-    bin_base = (lax.axis_index("chan") * tm_count + lax.axis_index("tm")) * per_dev
-    my_bins = lax.dynamic_slice_in_dim(bins, bin_base, per_dev, 0)
-    whole = beam(received, my_bins, positions, slow_index, scale)[:, :per_dev]
-    return lax.all_to_all(whole, "tm", split_axis=0, concat_axis=1, tiled=True)
+    )(my_bins, grid_rows(slow_index), bin_rows, twice, records)
+    return lax.all_to_all(picked[:, :per_dev], "tm", split_axis=0, concat_axis=1, tiled=True)
 
 
 def solution(mesh):

time: 175 us -> 91.1 us (0.52); the launches traced: 173 us -> 90.7 us
  blocking collectives: 74.3 us -> 7 us
  Pallas kernels: 36 us -> 79.4 us
  local copies, waits for them, and re-layouts: 24.7 us -> 2.55 us
  waiting for transfers between devices: 11.4 us -> 0 us
  matrix products: 10.5 us -> 0 us
  other arithmetic: 10.1 us -> 1.7 us
  starting transfers between devices: 5.33 us -> 0 us
    all_to_all x2 -> x1, blocking collectives: 59.7 us -> 7 us  [shards(): lax.all_to_all(picked[:, :per_dev], 'tm', split_axis=0, concat_axis=1, ti...]
    pallas_call x1, Pallas kernels: 36 us -> 79.4 us  [shards(): pl.pallas_call(functools.partial(kernel, scale, tm_count, chan_count), ou...]
    all_gather x1 -> x0, blocking collectives: 14.6 us -> none  [shards(): positions = lax.all_gather(coords, 'chan', axis=1, tiled=True)]
    all_to_all x1 -> x0, waiting for transfers between devices: 11.4 us -> none  [shards(): lax.all_to_all(lax.all_to_all(spectra, 'chan', split_axis=0, concat_axis=...]
    dot_general x3 -> x0, matrix products: 10.5 us -> none  [the longest x1 5.82 us: shards(): jnp.einsum('cnj,jq->qnc', blocks, table[:hop], preferred_element_type=jnp...]
    another operation x2 -> x0, other arithmetic: 10 us -> none
    all_to_all x4 -> x1, local copies, waits for them, and re-layouts: 9.56 us -> 0.29 us  [shards(): lax.all_to_all(picked[:, :per_dev], 'tm', split_axis=0, concat_axis=1, ti...]
    convert_element_type x1 -> x0, local copies, waits for them, and re-layouts: 6.64 us -> none  [shards(): (first + second).astype(jnp.bfloat16).reshape(2 * freq, snaps_dev * ch_dev)]
  transfers between devices with their start and end apart: 2 -> 0, of which waited for: 1 -> 0; matrix products, arithmetic and copies ran while one was open for 12% -> 0% of each run, Pallas kernels for 0% -> 0%
where the time goes in v2:
time: 91.1 us; the launch traced here: 90.7 us
  Pallas kernels  79.4 us (87%)
  blocking collectives  7 us (8%)
  local copies, waits for them, and re-layouts  2.55 us (3%)
  other arithmetic  1.7 us (2%)
    pallas_call x1, Pallas kernels, shards(): pl.pallas_call(functools.partial(kernel, scale, tm_count, chan_count), ou...  79.4 us
    all_to_all x1, blocking collectives, shards(): lax.all_to_all(picked[:, :per_dev], 'tm', split_axis=0, concat_axis=1, ti...  7 us

profile of v2, /device:TPU:10, one launch (start us, length us, event | category | flops | bytes accessed | tf_op | source)
XLA Modules:
  0.0 90.7 jit_solution(16478808405115036655)
XLA Ops:
  0.0 0.8 pad_add_fusion.coords_ref
  0.8 0.9 compare_select_fusion
  1.7 0.8 dynamic_slice.3.bins_ref
  2.5 0.8 broadcast_in_dim.12
  3.2 0.1 broadcast_in_dim_reshape.4.bin_rows
  3.3 79.4 %shard_map.46 = f32[2048,128]{1,0:T(8,128)S(1)} custom-call(s32[8]{0:T(128)S(1)} %dynamic_slice.3.bins_ref, s32[2048]{0:T(1024)S(1)} %bitcast.7, s32[512,1]{1,0:T(8,128)S(1)} %broadcast_in_dim_reshape.4.bin_rows, s32[2,128]{1,0:T(2,128)S(1)} %pad_add_fusion.coords_ref, bf16[64,32768]{1,0:T(8,128)(2,1)} %records_ref.1), custom_call_target="tpu_custom_call" | custom-call | flops 17179869184 | bytes 4194304 | tf_op jit(solution)/shard_map/pallas_call | solution.py:337
  82.8 0.3 copy.9
  83.1 7.0 %all_to_all.19 = f32[2,1024,8]{1,2,0:T(8,128)S(1)} all-to-all(f32[2,1024,8]{1,2,0:T(8,128)S(1)} %copy.9), channel_id=1, replica_groups=mesh['chan'=16,'tm'=2] {'tm'}, dimensions={0} | all-to-all | bytes 131072 | tf_op jit(solution)/shard_map/all_to_all | solution.py:372
  90.1 0.6 copy.11

commit v3 on v2

v3 whole, which is shorter than its diff:
```python
import functools
import math

import jax
import jax.numpy as jnp
import numpy as np
from jax import lax
from jax.experimental import pallas as pl
from jax.experimental.pallas import tpu as pltpu
from jax.sharding import PartitionSpec as P

W = 2048
REACH = 32
LANES = 128
INNER = 6
OUTER = 2
SPAN = 2 * INNER + 1
TURNS = 2 * OUTER + 1
CHUNKS = 4


def circle_fit():
    u = 0.125 * (1.0 - np.cos(math.pi * (np.arange(400) + 0.5) / 400))
    t = np.sqrt(u)
    powers = u[:, None] ** np.arange(6)[None, :]
    scaled = powers * (4.0 ** np.arange(6))
    cos_fit = np.linalg.lstsq(scaled, np.cos(2 * math.pi * t), rcond=None)[0]
    sin_fit = np.linalg.lstsq(scaled, np.sin(2 * math.pi * t) / t, rcond=None)[0]
    back = 4.0 ** np.arange(6)
    return [float(v) for v in cos_fit * back], [float(v) for v in sin_fit * back]


COS_FIT, SIN_FIT = circle_fit()


def horner(u, fit):
    total = jnp.full_like(u, fit[-1])
    for value in fit[-2::-1]:
        total = total * u + value
    return total


def circle(t):
    t = t - jnp.floor(t + 0.5)
    u = t * t
    return horner(u, COS_FIT), t * horner(u, SIN_FIT)


MAIN = TURNS * 4 * INNER * REACH
FLAT = MAIN + TURNS * 2 * REACH
GRID = FLAT + TURNS * 2 * 8


def grid_rows(slow_index):
    turn = (slow_index[0] + REACH) // SPAN
    inner = slow_index[0] - SPAN * (turn - OUTER)
    second = slow_index[1]
    low0, low1 = (inner < 0).astype(jnp.int32), (second < 0).astype(jnp.int32)
    a0, a1 = jnp.abs(inner), jnp.abs(second)
    quad = jnp.where(low0 == low1, 0, 2) + low0
    main = ((turn * 4 + quad) * INNER + a0 - 1) * REACH + a1 - 1
    on_second = MAIN + (turn * 2 + low1) * REACH + a1 - 1
    on_first = FLAT + (turn * 2 + low0) * 8 + a0
    return jnp.where(a1 == 0, on_first, jnp.where(a0 == 0, on_second, main))


def product(rows, columns):
    return lax.dot_general(
        rows, columns, (((1,), (1,)), ((), ())), preferred_element_type=jnp.float32
    )


def kernel(
    scale, tm_count, chan_count, bins_ref, pick_ref, coords_ref, records_ref, out_ref,
    blocks, table, stage, send, recv, digits, all_digits, positions,
    yt, yj, c0, s0, c1, s1, ra, rb, grid_power, picked, mine, swapped,
    load_sem, halo_sems, digit_sems, send_sems, recv_sems, power_sems,
):
    devices = tm_count * chan_count
    chunks, _, chunk_rows, _ = recv.shape
    ch_dev, local_samples = records_ref.shape
    hop = W // 2
    snaps = local_samples // hop
    tiles = snaps * ch_dev // LANES
    per_dev = bins_ref.shape[0] // devices
    per_chunk = per_dev // chunks
    freq_rows = table.shape[0]
    half = LANES // 2
    side = tm_count * 2 * tiles
    my_chan, my_tm = lax.axis_index("chan"), lax.axis_index("tm")
    me = my_chan * tm_count + my_tm
    lane = lax.broadcasted_iota(jnp.int32, (1, LANES), 1)
    mesh_id = pl.DeviceIdType.MESH

    barrier = pltpu.get_barrier_semaphore()

    def greet(j, _):
        other = lax.rem(me + j, devices)
        pl.semaphore_signal(
            barrier,
            inc=1,
            device_id=(lax.div(other, tm_count), lax.rem(other, tm_count)),
            device_id_type=mesh_id,
        )
        return 0

    lax.fori_loop(1, devices, greet, 0)

    def load(n, _):
        pltpu.make_async_copy(
            records_ref.at[:, pl.ds(pl.multiple_of(n * hop, hop), hop)],
            blocks.at[pl.ds(pl.multiple_of(n * ch_dev, ch_dev), ch_dev), :],
            load_sem,
        ).start()
        return 0

    lax.fori_loop(0, snaps, load, 0)
    digits[...] = jnp.zeros_like(digits)
    for axis in range(2):
        values = coords_ref[axis : axis + 1, :].astype(jnp.float32)
        high = jnp.floor(values * (1.0 / 32.0))
        digits[2 * axis : 2 * axis + 1, 0:ch_dev] = high.astype(digits.dtype)
        digits[2 * axis + 1 : 2 * axis + 2, 0:ch_dev] = (values - 32.0 * high).astype(digits.dtype)
    all_digits[my_chan] = digits[...]
    pl.semaphore_wait(barrier, devices - 1)

    halo = pltpu.make_async_remote_copy(
        src_ref=records_ref.at[:, 0:hop],
        dst_ref=blocks.at[snaps * ch_dev : (snaps + 1) * ch_dev, :],
        send_sem=halo_sems.at[0],
        recv_sem=halo_sems.at[1],
        device_id=(my_chan, lax.rem(my_tm + tm_count - 1, tm_count)),
        device_id_type=mesh_id,
    )
    halo.start()

    def tell(j, _):
        pltpu.make_async_remote_copy(
            src_ref=digits,
            dst_ref=all_digits.at[my_chan],
            send_sem=digit_sems.at[0],
            recv_sem=digit_sems.at[1],
            device_id=(lax.rem(my_chan + j, chan_count), my_tm),
            device_id_type=mesh_id,
        ).start()
        return 0

    lax.fori_loop(1, chan_count, tell, 0)

    offset = lax.broadcasted_iota(jnp.int32, (1, W), 1).astype(jnp.float32) * (1.0 / W)
    weight = (0.5 - 0.5 * circle(offset)[0]) * math.sqrt(8.0 / (3.0 * W))
    row16 = lax.broadcasted_iota(jnp.int32, (16, 1), 0)
    quarter = lax.rem(row16, 2).astype(jnp.float32) * 0.25

    def table_chunk(k):
        def table_rows(r, _):
            values = jnp.zeros((16, 1), jnp.float32)
            for i in range(8):
                b = r * 8 + i
                index = lax.div(b, per_chunk) * per_dev + k * per_chunk + lax.rem(b, per_chunk)
                values = jnp.where(row16 // 2 == i, bins_ref[index].astype(jnp.float32), values)
            turn = values * offset + quarter
            turn = turn - jnp.floor(turn + 0.5)
            rows = pl.ds(pl.multiple_of(r * 16, 16), 16)
            table[rows, :] = (weight * horner(turn * turn, COS_FIT)).astype(table.dtype)
            return 0

        lax.fori_loop(0, freq_rows // 16, table_rows, 0)

    table_chunk(0)
    whole = blocks.at[0 : snaps * ch_dev, :]
    pltpu.make_async_copy(whole, whole, load_sem).wait()
    halo.wait()
    tail = blocks[snaps * ch_dev :, :]
    blocks[snaps * ch_dev :, :] = jnp.where(my_tm == tm_count - 1, jnp.zeros_like(tail), tail)

    def part(d):
        return pl.ds(pl.multiple_of(d * chunk_rows, chunk_rows), chunk_rows)

    def send_chunk(k, _):
        def transform(i, _):
            start = pl.multiple_of(i * 2 * LANES, 2 * LANES)
            here = blocks[pl.ds(start, 2 * LANES), :]
            after = blocks[pl.ds(start + ch_dev, 2 * LANES), :]
            out = product(table[:, :hop], here) + product(table[:, hop:], after)
            for j in range(2):
                rows = pl.ds(2 * i + j, freq_rows, stride=tiles)
                stage[rows, :] = out[:, j * LANES : (j + 1) * LANES]
            return 0

        lax.fori_loop(0, tiles // 2, transform, 0)

        def pack(d, _):
            send[k, part(d), :] = stage[part(d), :].astype(send.dtype)
            return 0

        lax.fori_loop(0, devices, pack, 0)

        def send_one(j, _):
            other = lax.rem(me + j, devices)
            pltpu.make_async_remote_copy(
                src_ref=send.at[k, part(other), :],
                dst_ref=recv.at[k, me],
                send_sem=send_sems.at[k],
                recv_sem=recv_sems.at[k],
                device_id=(lax.div(other, tm_count), lax.rem(other, tm_count)),
                device_id_type=mesh_id,
            ).start()
            return 0

        lax.fori_loop(1, devices, send_one, 0)
        recv[k, me] = send[k, part(me), :]

        @pl.when(k + 1 < chunks)
        def _():
            table_chunk(k + 1)

        return 0

    lax.fori_loop(0, chunks, send_chunk, 0)

    others = all_digits.at[0 : chan_count - 1]
    pltpu.make_async_copy(others, others, digit_sems.at[1]).wait()
    pltpu.make_async_copy(others, others, digit_sems.at[0]).wait()
    for m in range(chan_count // 2):
        left = all_digits[2 * m].astype(jnp.float32)
        right = pltpu.roll(all_digits[2 * m + 1].astype(jnp.float32), half, 1)
        both = jnp.where(lane < half, left, right)
        for axis in range(2):
            high, low = both[2 * axis : 2 * axis + 1], both[2 * axis + 1 : 2 * axis + 2]
            positions[axis : axis + 1, m * LANES : (m + 1) * LANES] = 32.0 * high + low

    modulus = 5 * W // 2
    inner_step = lax.broadcasted_iota(jnp.int32, (8, 1), 0)
    inner_step = jnp.where(inner_step <= INNER, inner_step, SPAN).astype(jnp.float32)
    step = (lax.broadcasted_iota(jnp.int32, (REACH, 1), 0) + 1).astype(jnp.float32)

    def one_bin(k, local, _):
        f = k * per_chunk + local
        bin_value = bins_ref[me * per_dev + f].astype(jnp.float32)
        for axis, steps, cos_ref, sin_ref in ((0, inner_step, c0, s0), (1, step, c1, s1)):
            turn = positions[axis : axis + 1, :] * bin_value
            turn = (turn - modulus * jnp.floor(turn * (1.0 / modulus))) * (1.0 / modulus)
            turn = turn - jnp.floor(turn + 0.5)
            cosine, sine = circle(turn * steps)
            cos_ref[...] = cosine
            sin_ref[...] = sine
        for m in range(chan_count // 2):
            cols = slice(m * LANES, (m + 1) * LANES)
            cos_1, sin_1 = c0[INNER + 1 : INNER + 2, cols], s0[INNER + 1 : INNER + 2, cols]
            spins = [(cos_1, sin_1), (2.0 * cos_1 * cos_1 - 1.0, 2.0 * sin_1 * cos_1)]
            for t in range(tm_count):
                pairs = []
                for p in range(2):
                    rows = pl.ds(pl.multiple_of((2 * local + p) * tiles, tiles), tiles)
                    left = recv[k, 2 * m * tm_count + t, rows, :].astype(jnp.float32)
                    right = recv[k, (2 * m + 1) * tm_count + t, rows, :].astype(jnp.float32)
                    even = jnp.where(lane < half, left, pltpu.roll(right, half, 1))
                    odd = jnp.where(lane < half, pltpu.roll(left, half, 1), right)
                    pairs.append((even, odd))
                for parity in range(2):
                    re, im = pairs[0][parity], pairs[1][parity]
                    turned = [None] * TURNS
                    turned[OUTER] = (re, im)
                    for h, (cosine, sine) in enumerate(spins, 1):
                        cr, si, ci, sr = cosine * re, sine * im, cosine * im, sine * re
                        turned[OUTER + h] = (cr + si, ci - sr)
                        turned[OUTER - h] = (cr - si, ci + sr)
                    for h, (real, imag) in enumerate(turned):
                        top = 2 * side * h + (t * 2 + parity) * tiles
                        low = top + side
                        yt[top : top + tiles, cols] = real.astype(yt.dtype)
                        yt[low : low + tiles, cols] = imag.astype(yt.dtype)
                        yj[top : top + tiles, cols] = imag.astype(yj.dtype)
                        yj[low : low + tiles, cols] = (-real).astype(yj.dtype)

        def put(row, values):
            total = jnp.sum(values * values, axis=1, keepdims=True)
            rows = pl.ds(row, values.shape[0])
            grid_power[rows, :] = jnp.where(lane == f, total, grid_power[rows, :])

        cosines, sines = c1[...], s1[...]
        for l in range(INNER):
            cos_row, sin_row = c0[l + 1 : l + 2, :], s0[l + 1 : l + 2, :]
            at = 2 * REACH * l
            ra[at : at + REACH, :] = (cos_row * cosines).astype(ra.dtype)
            ra[at + REACH : at + 2 * REACH, :] = (sin_row * sines).astype(ra.dtype)
            rb[at : at + REACH, :] = (sin_row * cosines).astype(rb.dtype)
            rb[at + REACH : at + 2 * REACH, :] = (cos_row * sines).astype(rb.dtype)
        edge = 2 * REACH * INNER
        ra[edge : edge + REACH, :] = cosines.astype(ra.dtype)
        rb[edge : edge + REACH, :] = sines.astype(rb.dtype)
        flat = edge + REACH
        ra[flat : flat + 16, :] = jnp.concatenate([c0[...]] * 2, axis=0).astype(ra.dtype)
        rb[flat : flat + 16, :] = jnp.concatenate([s0[...]] * 2, axis=0).astype(rb.dtype)
        for first in range(0, TURNS, 2):
            turns = range(first, min(first + 2, TURNS))
            columns = slice(2 * side * turns[0], 2 * side * (turns[-1] + 1))
            da = product(ra[...], yt[columns, :])
            db = product(rb[...], yj[columns, :])
            for h in turns:
                lanes = slice(2 * side * (h - first), 2 * side * (h - first + 1))
                for l in range(INNER):
                    at = 2 * REACH * l
                    cc, ss = da[at : at + REACH, lanes], da[at + REACH : at + 2 * REACH, lanes]
                    sc, cs = db[at : at + REACH, lanes], db[at + REACH : at + 2 * REACH, lanes]
                    even_same, even_other = cc - ss, cc + ss
                    odd_same, odd_other = sc + cs, sc - cs
                    row, step_rows = (h * 4 * INNER + l) * REACH, INNER * REACH
                    put(row, even_same + odd_same)
                    put(row + step_rows, even_same - odd_same)
                    put(row + 2 * step_rows, even_other + odd_other)
                    put(row + 3 * step_rows, even_other - odd_other)
                even, odd = da[edge:flat, lanes], db[edge:flat, lanes]
                put(MAIN + 2 * h * REACH, even + odd)
                put(MAIN + (2 * h + 1) * REACH, even - odd)
                even, odd = da[flat : flat + 8, lanes], db[flat : flat + 8, lanes]
                put(FLAT + 16 * h, even + odd)
                put(FLAT + 16 * h + 8, even - odd)
        return 0

    grid_power[...] = jnp.zeros_like(grid_power)

    def one_chunk(k, _):
        arrived = recv.at[k, 0 : devices - 1]
        pltpu.make_async_copy(arrived, arrived, recv_sems.at[k]).wait()
        lax.fori_loop(0, per_chunk, functools.partial(one_bin, k), 0)
        return 0

    lax.fori_loop(0, chunks, one_chunk, 0)

    def pick(block, _):
        start = pl.multiple_of(block * 8, 8)
        for k in range(8):
            picked[pl.ds(start + k, 1), :] = grid_power[pl.ds(pick_ref[start + k], 1), :] * scale
        return 0

    lax.fori_loop(0, picked.shape[0] // 8, pick, 0)
    kept = mine.shape[1]
    own = mine.shape[2]
    for t in range(tm_count):
        for b in range(own // LANES):
            start = t * own + b * LANES
            turned = picked[start : start + LANES, :].T
            mine[t, :, b * LANES : (b + 1) * LANES] = turned[:kept, :]
    exchanges = []
    for j in range(1, tm_count):
        other = lax.rem(my_tm + j, tm_count)
        copy = pltpu.make_async_remote_copy(
            src_ref=mine.at[other],
            dst_ref=swapped.at[my_tm],
            send_sem=power_sems.at[0, j - 1],
            recv_sem=power_sems.at[1, j - 1],
            device_id=(my_chan, other),
            device_id_type=mesh_id,
        )
        copy.start()
        exchanges.append(copy)
    swapped[my_tm] = mine[my_tm]
    for copy in exchanges:
        copy.wait()
    out_ref[...] = swapped[...]

    def drain(k, _):
        sent = send.at[k, 0 : (devices - 1) * chunk_rows, :]
        pltpu.make_async_copy(sent, sent, send_sems.at[k]).wait()
        return 0

    lax.fori_loop(0, chunks, drain, 0)


def shards(records, coords, bins, slow_index):
    ch_dev, local_samples = records.shape
    hop = W // 2
    snaps = local_samples // hop
    chan_count = lax.axis_size("chan")
    tm_count = lax.axis_size("tm")
    devices = chan_count * tm_count
    channels = ch_dev * chan_count
    freq = bins.shape[0]
    per_dev = freq // devices
    chunks = math.gcd(per_dev, CHUNKS)
    tiles = snaps * ch_dev // LANES
    chunk_rows = 2 * per_dev * tiles // chunks
    columns = TURNS * 4 * tm_count * tiles
    side_rows = 2 * REACH * INNER + REACH + 16
    kept = 8 * ((per_dev + 7) // 8)
    own = slow_index.shape[1] // tm_count
    scale = 1.0 / (channels * snaps * tm_count)
    vmem = pl.BlockSpec(memory_space=pltpu.VMEM)
    smem = pl.BlockSpec(memory_space=pltpu.SMEM)
    inner_angles = pltpu.VMEM((8, channels), jnp.float32)
    angles = pltpu.VMEM((REACH, channels), jnp.float32)
    power = pl.pallas_call(
        functools.partial(kernel, scale, tm_count, chan_count),
        out_shape=jax.ShapeDtypeStruct((tm_count, kept, own), jnp.float32),
        in_specs=[smem, smem, vmem, pl.BlockSpec(memory_space=pl.ANY)],
        out_specs=vmem,
        scratch_shapes=[
            pltpu.VMEM(((snaps + 1) * ch_dev, hop), jnp.bfloat16),
            pltpu.VMEM((2 * freq // chunks, W), jnp.bfloat16),
            pltpu.VMEM((2 * freq * tiles // chunks, LANES), jnp.float32),
            pltpu.VMEM((chunks, devices * chunk_rows, LANES), jnp.bfloat16),
            pltpu.VMEM((chunks, devices, chunk_rows, LANES), jnp.bfloat16),
            pltpu.VMEM((16, LANES), jnp.bfloat16),
            pltpu.VMEM((chan_count, 16, LANES), jnp.bfloat16),
            pltpu.VMEM((2, channels), jnp.float32),
            pltpu.VMEM((columns, channels), jnp.bfloat16),
            pltpu.VMEM((columns, channels), jnp.bfloat16),
            inner_angles, inner_angles, angles, angles,
            pltpu.VMEM((side_rows, channels), jnp.bfloat16),
            pltpu.VMEM((side_rows, channels), jnp.bfloat16),
            pltpu.VMEM((GRID, LANES), jnp.float32),
            pltpu.VMEM((slow_index.shape[1], LANES), jnp.float32),
            pltpu.VMEM((tm_count, kept, own), jnp.float32),
            pltpu.VMEM((tm_count, kept, own), jnp.float32),
            pltpu.SemaphoreType.DMA,
            pltpu.SemaphoreType.DMA((2,)),
            pltpu.SemaphoreType.DMA((2,)),
            pltpu.SemaphoreType.DMA((chunks,)),
            pltpu.SemaphoreType.DMA((chunks,)),
            pltpu.SemaphoreType.DMA((2, tm_count)),
        ],
        compiler_params=pltpu.CompilerParams(
            collective_id=0, has_side_effects=True, vmem_limit_bytes=52 * 2**20
        ),
        cost_estimate=pl.CostEstimate(
            flops=4 * side_rows * columns * channels * per_dev,
            bytes_accessed=records.size * 2,
            transcendentals=0,
        ),
    )(bins, grid_rows(slow_index), coords, records)
    return power[:, :per_dev, :].reshape(tm_count * per_dev, own).T


def solution(mesh):
    return jax.shard_map(
        shards,
        mesh=mesh,
        in_specs=(P("chan", "tm"), P(None, "chan"), P(), P()),
        out_specs=P("tm", "chan"),
        check_vma=False,
    )
```

time: 91.1 us -> 75.6 us (0.83)
  Pallas kernels: 79.4 us -> 71.6 us
  blocking collectives: 7 us -> 0 us
    pallas_call x1, Pallas kernels: 79.4 us -> 71.6 us  [shards(): pl.pallas_call(functools.partial(kernel, scale, tm_count, chan_count), ou...]
    all_to_all x1 -> x0, blocking collectives: 7 us -> none  [shards(): lax.all_to_all(picked[:, :per_dev], 'tm', split_axis=0, concat_axis=1, ti...]
    unnamed x1 -> x5, local copies, waits for them, and re-layouts: 0.63 us -> 1.98 us
where the time goes in v3:
time: 75.6 us; the launch traced here: 75.1 us
  Pallas kernels  71.6 us (95%)
  local copies, waits for them, and re-layouts  1.98 us (3%)
  other arithmetic  1.57 us (2%)
    pallas_call x1, Pallas kernels, shards(): pl.pallas_call(functools.partial(kernel, scale, tm_count, chan_count), ou...  71.6 us
    unnamed x5, local copies, waits for them, and re-layouts  1.98 us

profile of v3, /device:TPU:10, one launch (start us, length us, event | category | flops | bytes accessed | tf_op | source)
XLA Modules:
  0.0 75.1 jit_solution(2980660098328369695)
XLA Ops:
  0.0 0.7 compare_convert_fusion
  0.7 0.8 %fusion.13 = (s32[1,2048]{1,0:T(1,128)S(1)}, s32[1,2048]{1,0:T(1,128)S(1)}) fusion(s32[2,2048]{1,0:T(2,128)} %param.7), kind=kLoop, calls=%fused_computation.22 | loop fusion | flops 2048 | bytes 32768 | tf_op jit(solution)/shard_map/slice | solution.py:55
  1.6 0.0 copy-start
  1.6 0.7 copy-done
  2.3 0.0 copy-start.1
  2.3 0.7 copy-done.1
  2.9 71.6 %shard_map.46 = f32[2,8,1024]{2,1,0:T(8,128)S(1)} custom-call(s32[256]{0:T(256)S(1)} %copy-done, s32[2048]{0:T(1024)S(1)} %fusion.3.pick_ref, s32[2,64]{1,0:T(2,128)S(1)} %copy-done.1, bf16[64,32768]{1,0:T(8,128)(2,1)} %records_ref.1), custom_call_target="tpu_custom_call" | custom-call | flops 9059696640 | bytes 4194304 | tf_op jit(solution)/shard_map/pallas_call | solution.py:394
  74.5 0.6 copy.6
  (1 shorter events, 0.0 us)
Async XLA Ops:
  1.6 0.7 copy-start
  2.3 0.7 copy-start.1

commit v4 on v3

--- a/solution.py
+++ b/solution.py
@@ -46,22 +46,22 @@
     return horner(u, COS_FIT), t * horner(u, SIN_FIT)
 
 
-MAIN = TURNS * 4 * INNER * REACH
-FLAT = MAIN + TURNS * 2 * REACH
-GRID = FLAT + TURNS * 2 * 8
-
-
-def grid_rows(slow_index):
-    turn = (slow_index[0] + REACH) // SPAN
-    inner = slow_index[0] - SPAN * (turn - OUTER)
-    second = slow_index[1]
+SECOND = INNER * REACH
+FIRST = SECOND + REACH
+SET = 2 * LANES
+POINTS = 8 * ((4 * TURNS + 7) // 8)
+
+
+def grid_place(slow_index):
+    first, second = slow_index[0:1, :], slow_index[1:2, :]
+    turn = sum((first + REACH >= SPAN * h).astype(jnp.int32) for h in range(1, TURNS))
+    inner = first - SPAN * (turn - OUTER)
     low0, low1 = (inner < 0).astype(jnp.int32), (second < 0).astype(jnp.int32)
     a0, a1 = jnp.abs(inner), jnp.abs(second)
-    quad = jnp.where(low0 == low1, 0, 2) + low0
-    main = ((turn * 4 + quad) * INNER + a0 - 1) * REACH + a1 - 1
-    on_second = MAIN + (turn * 2 + low1) * REACH + a1 - 1
-    on_first = FLAT + (turn * 2 + low0) * 8 + a0
-    return jnp.where(a1 == 0, on_first, jnp.where(a0 == 0, on_second, main))
+    quad = jnp.where(low0 == low1, low0, 2 + low0)
+    quad = jnp.where(a0 == 0, low1, jnp.where(a1 == 0, low0, quad))
+    lane = jnp.where(a0 == 0, SECOND + a1 - 1, (a0 - 1) * REACH + a1 - 1)
+    return turn * 4 + quad, jnp.where(a1 == 0, FIRST + a0, lane)
 
 
 def product(rows, columns):
@@ -71,9 +71,9 @@
 
 
 def kernel(
-    scale, tm_count, chan_count, bins_ref, pick_ref, coords_ref, records_ref, out_ref,
+    scale, tm_count, chan_count, bins_ref, slow_ref, coords_ref, records_ref, out_ref,
     blocks, table, stage, send, recv, digits, all_digits, positions,
-    yt, yj, c0, s0, c1, s1, ra, rb, grid_power, picked, mine, swapped,
+    yt, yj, c0, s0, c1, s1, sets, dots, power, place, onehot, mine, swapped,
     load_sem, halo_sems, digit_sems, send_sems, recv_sems, power_sems,
 ):
     devices = tm_count * chan_count
@@ -170,15 +170,28 @@
     table_chunk(0)
     whole = blocks.at[0 : snaps * ch_dev, :]
     pltpu.make_async_copy(whole, whole, load_sem).wait()
-    halo.wait()
-    tail = blocks[snaps * ch_dev :, :]
-    blocks[snaps * ch_dev :, :] = jnp.where(my_tm == tm_count - 1, jnp.zeros_like(tail), tail)
 
     def part(d):
         return pl.ds(pl.multiple_of(d * chunk_rows, chunk_rows), chunk_rows)
 
+    def partner(j):
+        if devices & (devices - 1):
+            return lax.rem(me + j, devices)
+        other = me
+        for b in range(devices.bit_length() - 1):
+            flip = 1 - 2 * lax.rem(lax.div(me, 2**b), 2)
+            other = other + lax.rem(lax.div(j, 2**b), 2) * flip * 2**b
+        return other
+
     def send_chunk(k, _):
         def transform(i, _):
+            @pl.when(jnp.logical_and(k == 0, i == tiles // 2 - 1))
+            def _():
+                halo.wait()
+                tail = blocks[snaps * ch_dev :, :]
+                last = my_tm == tm_count - 1
+                blocks[snaps * ch_dev :, :] = jnp.where(last, jnp.zeros_like(tail), tail)
+
             start = pl.multiple_of(i * 2 * LANES, 2 * LANES)
             here = blocks[pl.ds(start, 2 * LANES), :]
             after = blocks[pl.ds(start + ch_dev, 2 * LANES), :]
@@ -197,7 +210,7 @@
         lax.fori_loop(0, devices, pack, 0)
 
         def send_one(j, _):
-            other = lax.rem(me + j, devices)
+            other = partner(devices - j)
             pltpu.make_async_remote_copy(
                 src_ref=send.at[k, part(other), :],
                 dst_ref=recv.at[k, me],
@@ -218,6 +231,14 @@
         return 0
 
     lax.fori_loop(0, chunks, send_chunk, 0)
+
+    point, spot = grid_place(slow_ref[...])
+    place[...] = point
+    for first in range(0, SET, 16):
+        row = lax.broadcasted_iota(jnp.int32, (16, 1), 0) + first
+        onehot[first : first + 16, :] = (row == spot).astype(jnp.float32).astype(onehot.dtype)
+    sets[...] = jnp.zeros_like(sets)
+    power[...] = jnp.zeros_like(power)
 
     others = all_digits.at[0 : chan_count - 1]
     pltpu.make_async_copy(others, others, digit_sems.at[1]).wait()
@@ -274,52 +295,32 @@
                         yj[top : top + tiles, cols] = imag.astype(yj.dtype)
                         yj[low : low + tiles, cols] = (-real).astype(yj.dtype)
 
-        def put(row, values):
-            total = jnp.sum(values * values, axis=1, keepdims=True)
-            rows = pl.ds(row, values.shape[0])
-            grid_power[rows, :] = jnp.where(lane == f, total, grid_power[rows, :])
-
         cosines, sines = c1[...], s1[...]
         for l in range(INNER):
             cos_row, sin_row = c0[l + 1 : l + 2, :], s0[l + 1 : l + 2, :]
-            at = 2 * REACH * l
-            ra[at : at + REACH, :] = (cos_row * cosines).astype(ra.dtype)
-            ra[at + REACH : at + 2 * REACH, :] = (sin_row * sines).astype(ra.dtype)
-            rb[at : at + REACH, :] = (sin_row * cosines).astype(rb.dtype)
-            rb[at + REACH : at + 2 * REACH, :] = (cos_row * sines).astype(rb.dtype)
-        edge = 2 * REACH * INNER
-        ra[edge : edge + REACH, :] = cosines.astype(ra.dtype)
-        rb[edge : edge + REACH, :] = sines.astype(rb.dtype)
-        flat = edge + REACH
-        ra[flat : flat + 16, :] = jnp.concatenate([c0[...]] * 2, axis=0).astype(ra.dtype)
-        rb[flat : flat + 16, :] = jnp.concatenate([s0[...]] * 2, axis=0).astype(rb.dtype)
-        for first in range(0, TURNS, 2):
-            turns = range(first, min(first + 2, TURNS))
-            columns = slice(2 * side * turns[0], 2 * side * (turns[-1] + 1))
-            da = product(ra[...], yt[columns, :])
-            db = product(rb[...], yj[columns, :])
-            for h in turns:
-                lanes = slice(2 * side * (h - first), 2 * side * (h - first + 1))
-                for l in range(INNER):
-                    at = 2 * REACH * l
-                    cc, ss = da[at : at + REACH, lanes], da[at + REACH : at + 2 * REACH, lanes]
-                    sc, cs = db[at : at + REACH, lanes], db[at + REACH : at + 2 * REACH, lanes]
-                    even_same, even_other = cc - ss, cc + ss
-                    odd_same, odd_other = sc + cs, sc - cs
-                    row, step_rows = (h * 4 * INNER + l) * REACH, INNER * REACH
-                    put(row, even_same + odd_same)
-                    put(row + step_rows, even_same - odd_same)
-                    put(row + 2 * step_rows, even_other + odd_other)
-                    put(row + 3 * step_rows, even_other - odd_other)
-                even, odd = da[edge:flat, lanes], db[edge:flat, lanes]
-                put(MAIN + 2 * h * REACH, even + odd)
-                put(MAIN + (2 * h + 1) * REACH, even - odd)
-                even, odd = da[flat : flat + 8, lanes], db[flat : flat + 8, lanes]
-                put(FLAT + 16 * h, even + odd)
-                put(FLAT + 16 * h + 8, even - odd)
-        return 0
-
-    grid_power[...] = jnp.zeros_like(grid_power)
+            rows = slice(l * REACH, (l + 1) * REACH)
+            sets[0, rows, :] = (cos_row * cosines).astype(sets.dtype)
+            sets[1, rows, :] = (sin_row * sines).astype(sets.dtype)
+            sets[2, rows, :] = (sin_row * cosines).astype(sets.dtype)
+            sets[3, rows, :] = (cos_row * sines).astype(sets.dtype)
+        sets[0, SECOND:FIRST, :] = cosines.astype(sets.dtype)
+        sets[3, SECOND:FIRST, :] = sines.astype(sets.dtype)
+        flat = slice(FIRST, FIRST + 16)
+        sets[0, flat, :] = jnp.concatenate([c0[...]] * 2, axis=0).astype(sets.dtype)
+        sets[2, flat, :] = jnp.concatenate([s0[...]] * 2, axis=0).astype(sets.dtype)
+        for q in range(4):
+            dots[q] = product((yt if q < 2 else yj)[...], sets[q])
+        for h in range(TURNS):
+            rows = slice(2 * side * h, 2 * side * (h + 1))
+            cc, ss, sc, cs = dots[0, rows, :], dots[1, rows, :], dots[2, rows, :], dots[3, rows, :]
+            even_same, even_other = cc - ss, cc + ss
+            odd_same, odd_other = sc + cs, sc - cs
+            for q, value in enumerate(
+                (even_same + odd_same, even_same - odd_same, even_other + odd_other, even_other - odd_other)
+            ):
+                total = jnp.sum(value * value, axis=0, keepdims=True)
+                power[pl.ds(f * POINTS + 4 * h + q, 1), :] = total * scale
+        return 0
 
     def one_chunk(k, _):
         arrived = recv.at[k, 0 : devices - 1]
@@ -329,20 +330,18 @@
 
     lax.fori_loop(0, chunks, one_chunk, 0)
 
-    def pick(block, _):
-        start = pl.multiple_of(block * 8, 8)
-        for k in range(8):
-            picked[pl.ds(start + k, 1), :] = grid_power[pl.ds(pick_ref[start + k], 1), :] * scale
-        return 0
-
-    lax.fori_loop(0, picked.shape[0] // 8, pick, 0)
-    kept = mine.shape[1]
+    high = power[...].astype(jnp.bfloat16)
+    rest = (power[...] - high.astype(jnp.float32)).astype(jnp.bfloat16)
+    point_row = lax.broadcasted_iota(jnp.int32, (POINTS, 1), 0)
     own = mine.shape[2]
     for t in range(tm_count):
-        for b in range(own // LANES):
-            start = t * own + b * LANES
-            turned = picked[start : start + LANES, :].T
-            mine[t, :, b * LANES : (b + 1) * LANES] = turned[:kept, :]
+        cols = slice(t * own, (t + 1) * own)
+        spread = jnp.dot(high, onehot[:, cols], preferred_element_type=jnp.float32)
+        spread += jnp.dot(rest, onehot[:, cols], preferred_element_type=jnp.float32)
+        here = point_row == place[:, cols]
+        for f in range(per_dev):
+            rows = spread[f * POINTS : (f + 1) * POINTS]
+            mine[t, f : f + 1, :] = jnp.sum(jnp.where(here, rows, 0.0), axis=0, keepdims=True)
     exchanges = []
     for j in range(1, tm_count):
         other = lax.rem(my_tm + j, tm_count)
@@ -383,7 +382,6 @@
     tiles = snaps * ch_dev // LANES
     chunk_rows = 2 * per_dev * tiles // chunks
     columns = TURNS * 4 * tm_count * tiles
-    side_rows = 2 * REACH * INNER + REACH + 16
     kept = 8 * ((per_dev + 7) // 8)
     own = slow_index.shape[1] // tm_count
     scale = 1.0 / (channels * snaps * tm_count)
@@ -394,7 +392,7 @@
     power = pl.pallas_call(
         functools.partial(kernel, scale, tm_count, chan_count),
         out_shape=jax.ShapeDtypeStruct((tm_count, kept, own), jnp.float32),
-        in_specs=[smem, smem, vmem, pl.BlockSpec(memory_space=pl.ANY)],
+        in_specs=[smem, vmem, vmem, pl.BlockSpec(memory_space=pl.ANY)],
         out_specs=vmem,
         scratch_shapes=[
             pltpu.VMEM(((snaps + 1) * ch_dev, hop), jnp.bfloat16),
@@ -408,10 +406,11 @@
             pltpu.VMEM((columns, channels), jnp.bfloat16),
             pltpu.VMEM((columns, channels), jnp.bfloat16),
             inner_angles, inner_angles, angles, angles,
-            pltpu.VMEM((side_rows, channels), jnp.bfloat16),
-            pltpu.VMEM((side_rows, channels), jnp.bfloat16),
-            pltpu.VMEM((GRID, LANES), jnp.float32),
-            pltpu.VMEM((slow_index.shape[1], LANES), jnp.float32),
+            pltpu.VMEM((4, SET, channels), jnp.bfloat16),
+            pltpu.VMEM((4, columns, SET), jnp.float32),
+            pltpu.VMEM((per_dev * POINTS, SET), jnp.float32),
+            pltpu.VMEM((1, slow_index.shape[1]), jnp.int32),
+            pltpu.VMEM((SET, slow_index.shape[1]), jnp.bfloat16),
             pltpu.VMEM((tm_count, kept, own), jnp.float32),
             pltpu.VMEM((tm_count, kept, own), jnp.float32),
             pltpu.SemaphoreType.DMA,
@@ -425,11 +424,11 @@
             collective_id=0, has_side_effects=True, vmem_limit_bytes=52 * 2**20
         ),
         cost_estimate=pl.CostEstimate(
-            flops=4 * side_rows * columns * channels * per_dev,
+            flops=8 * SET * columns * channels * per_dev,
             bytes_accessed=records.size * 2,
             transcendentals=0,
         ),
-    )(bins, grid_rows(slow_index), coords, records)
+    )(bins, slow_index, coords, records)
     return power[:, :per_dev, :].reshape(tm_count * per_dev, own).T
 
 

time: 75.6 us -> 71.2 us (0.942)
  the two profiles are of different devices: /device:TPU:10 before, /device:TPU:0 now
where the time goes in v4:
time: 71.2 us; the launch traced here: 70.9 us
  Pallas kernels  68.2 us (96%)
  local copies, waits for them, and re-layouts  2.71 us (4%)
    pallas_call x1, Pallas kernels, shards(): pl.pallas_call(functools.partial(kernel, scale, tm_count, chan_count), ou...  68.2 us
    unnamed x7, local copies, waits for them, and re-layouts  2.71 us

profile of v4, /device:TPU:0, one launch (start us, length us, event | category | flops | bytes accessed | tf_op | source)
XLA Modules:
  0.0 70.9 jit_solution(10447287593567344527)
XLA Ops:
  0.0 0.0 copy-start
  0.0 0.7 %copy-done = s32[2,2048]{1,0:T(2,128)S(1)} copy-done((s32[2,2048]{1,0:T(2,128)S(1)}, s32[2,2048]{1,0:T(2,128)}, u32[]{:S(2)}) %copy-start) | copy-done | bytes 16408
  0.7 0.0 copy-start.1
  0.7 0.7 copy-done.1
  1.4 0.0 copy-start.2
  1.4 0.7 copy-done.2
  2.1 68.2 %shard_map.46 = f32[2,8,1024]{2,1,0:T(8,128)S(1)} custom-call(s32[256]{0:T(256)S(1)} %copy-done.1, s32[2,2048]{1,0:T(2,128)S(1)} %copy-done, s32[2,64]{1,0:T(2,128)S(1)} %copy-done.2, bf16[64,32768]{1,0:T(8,128)(2,1)} %records_ref.1), custom_call_target="tpu_custom_call" | custom-call | flops 10737418240 | bytes 4194304 | tf_op jit(solution)/shard_map/pallas_call | solution.py:392
  70.3 0.6 copy.6
Async XLA Ops:
  0.0 0.7 %copy-start = (s32[2,2048]{1,0:T(2,128)S(1)}, s32[2,2048]{1,0:T(2,128)}, u32[]{:S(2)}) copy-start(s32[2,2048]{1,0:T(2,128)} %slow_ref.1) | copy-start | bytes 49156
  0.7 0.7 copy-start.1
  1.4 0.7 copy-start.2

commit v5 on v4

--- a/solution.py
+++ b/solution.py
@@ -16,7 +16,7 @@
 OUTER = 2
 SPAN = 2 * INNER + 1
 TURNS = 2 * OUTER + 1
-CHUNKS = 4
+CHUNKS = 8
 
 
 def circle_fit():
@@ -71,10 +71,11 @@
 
 
 def kernel(
-    scale, tm_count, chan_count, bins_ref, slow_ref, coords_ref, records_ref, out_ref,
+    scale, tm_count, chan_count, bins_in, slow_in, coords_in, records_ref, out_ref,
+    bins_ref, slow_ref, coords_ref,
     blocks, table, stage, send, recv, digits, all_digits, positions,
     yt, yj, c0, s0, c1, s1, sets, dots, power, place, onehot, mine, swapped,
-    load_sem, halo_sems, digit_sems, send_sems, recv_sems, power_sems,
+    load_sem, small_sems, halo_sems, digit_sems, send_sems, recv_sems, power_sems,
 ):
     devices = tm_count * chan_count
     chunks, _, chunk_rows, _ = recv.shape
@@ -106,6 +107,15 @@
 
     lax.fori_loop(1, devices, greet, 0)
 
+    small = [
+        pltpu.make_async_copy(source, target, small_sems.at[i])
+        for i, (source, target) in enumerate(
+            ((coords_in, coords_ref), (bins_in, bins_ref), (slow_in, slow_ref))
+        )
+    ]
+    for copy in small:
+        copy.start()
+
     def load(n, _):
         pltpu.make_async_copy(
             records_ref.at[:, pl.ds(pl.multiple_of(n * hop, hop), hop)],
@@ -116,6 +126,8 @@
 
     lax.fori_loop(0, snaps, load, 0)
     digits[...] = jnp.zeros_like(digits)
+    for copy in small:
+        copy.wait()
     for axis in range(2):
         values = coords_ref[axis : axis + 1, :].astype(jnp.float32)
         high = jnp.floor(values * (1.0 / 32.0))
@@ -386,15 +398,17 @@
     own = slow_index.shape[1] // tm_count
     scale = 1.0 / (channels * snaps * tm_count)
     vmem = pl.BlockSpec(memory_space=pltpu.VMEM)
-    smem = pl.BlockSpec(memory_space=pltpu.SMEM)
     inner_angles = pltpu.VMEM((8, channels), jnp.float32)
     angles = pltpu.VMEM((REACH, channels), jnp.float32)
     power = pl.pallas_call(
         functools.partial(kernel, scale, tm_count, chan_count),
         out_shape=jax.ShapeDtypeStruct((tm_count, kept, own), jnp.float32),
-        in_specs=[smem, vmem, vmem, pl.BlockSpec(memory_space=pl.ANY)],
+        in_specs=[pl.BlockSpec(memory_space=pl.ANY)] * 4,
         out_specs=vmem,
         scratch_shapes=[
+            pltpu.SMEM(bins.shape, jnp.int32),
+            pltpu.VMEM(slow_index.shape, jnp.int32),
+            pltpu.VMEM(coords.shape, jnp.int32),
             pltpu.VMEM(((snaps + 1) * ch_dev, hop), jnp.bfloat16),
             pltpu.VMEM((2 * freq // chunks, W), jnp.bfloat16),
             pltpu.VMEM((2 * freq * tiles // chunks, LANES), jnp.float32),
@@ -414,6 +428,7 @@
             pltpu.VMEM((tm_count, kept, own), jnp.float32),
             pltpu.VMEM((tm_count, kept, own), jnp.float32),
             pltpu.SemaphoreType.DMA,
+            pltpu.SemaphoreType.DMA((3,)),
             pltpu.SemaphoreType.DMA((2,)),
             pltpu.SemaphoreType.DMA((2,)),
             pltpu.SemaphoreType.DMA((chunks,)),

time: 71.2 us -> 78 us (1.096)
  Pallas kernels: 68.2 us -> 75.1 us
    pallas_call x1, Pallas kernels: 68.2 us -> 75.1 us  [shards(): pl.pallas_call(functools.partial(kernel, scale, tm_count, chan_count), ou...]
where the time goes in v5:
time: 78 us; the launch traced here: 77.8 us
  Pallas kernels  75.1 us (96%)
  local copies, waits for them, and re-layouts  2.71 us (3%)
    pallas_call x1, Pallas kernels, shards(): pl.pallas_call(functools.partial(kernel, scale, tm_count, chan_count), ou...  75.1 us
    unnamed x7, local copies, waits for them, and re-layouts  2.71 us

profile of v5, /device:TPU:0, one launch (start us, length us, event | category | flops | bytes accessed | tf_op | source)
XLA Modules:
  0.0 77.8 jit_solution(3545082866363529832)
XLA Ops:
  0.0 0.0 copy-start
  0.0 0.7 copy-done
  0.7 0.0 copy-start.1
  0.7 0.7 copy-done.1
  1.4 0.0 copy-start.2
  1.4 0.7 copy-done.2
  2.1 75.1 %shard_map.46 = f32[2,8,1024]{2,1,0:T(8,128)S(1)} custom-call(s32[256]{0:T(256)S(1)} %copy-done.1, s32[2,2048]{1,0:T(2,128)S(1)} %copy-done, s32[2,64]{1,0:T(2,128)S(1)} %copy-done.2, bf16[64,32768]{1,0:T(8,128)(2,1)} %records_ref.1), custom_call_target="tpu_custom_call" | custom-call | flops 10737418240 | bytes 4194304 | tf_op jit(solution)/shard_map/pallas_call | solution.py:403
  77.2 0.6 copy.6
Async XLA Ops:
  0.0 0.7 copy-start
  0.7 0.7 copy-start.1
  1.4 0.7 copy-start.2

commit v6 on v5

--- a/solution.py
+++ b/solution.py
@@ -16,7 +16,7 @@
 OUTER = 2
 SPAN = 2 * INNER + 1
 TURNS = 2 * OUTER + 1
-CHUNKS = 8
+CHUNKS = 4
 
 
 def circle_fit():
@@ -222,7 +222,7 @@
         lax.fori_loop(0, devices, pack, 0)
 
         def send_one(j, _):
-            other = partner(devices - j)
+            other = partner(j // 2 + lax.rem(j, 2) * (devices // 2))
             pltpu.make_async_remote_copy(
                 src_ref=send.at[k, part(other), :],
                 dst_ref=recv.at[k, me],
@@ -436,7 +436,7 @@
             pltpu.SemaphoreType.DMA((2, tm_count)),
         ],
         compiler_params=pltpu.CompilerParams(
-            collective_id=0, has_side_effects=True, vmem_limit_bytes=52 * 2**20
+            collective_id=0, has_side_effects=True, vmem_limit_bytes=63 * 2**20
         ),
         cost_estimate=pl.CostEstimate(
             flops=8 * SET * columns * channels * per_dev,

time: 78 us -> 67.4 us (0.86)
  the two profiles are of different devices: /device:TPU:0 before, /device:TPU:10 now
where the time goes in v6:
time: 67.4 us; the launch traced here: 67.2 us
  Pallas kernels  65.8 us (98%)
  local copies, waits for them, and re-layouts  1.47 us (2%)
    pallas_call x1, Pallas kernels, shards(): pl.pallas_call(functools.partial(kernel, scale, tm_count, chan_count), ou...  65.8 us
    unnamed x1, local copies, waits for them, and re-layouts  1.47 us

profile of v6, /device:TPU:10, one launch (start us, length us, event | category | flops | bytes accessed | tf_op | source)
XLA Modules:
  0.0 67.2 jit_solution(9537520321370733522)
XLA Ops:
  0.0 65.8 %shard_map.46 = f32[2,8,1024]{2,1,0:T(8,128)} custom-call(s32[256]{0:T(256)} %bins_in.1, s32[2,2048]{1,0:T(2,128)} %slow_in.1, s32[2,64]{1,0:T(2,128)} %coords_in.1, bf16[64,32768]{1,0:T(8,128)(2,1)} %records_ref.1), custom_call_target="tpu_custom_call" | custom-call | flops 10737418240 | bytes 4194304 | tf_op jit(solution)/shard_map/pallas_call | solution.py:403
  65.8 1.5 %copy.6 = f32[1024,16]{0,1:T(8,128)} copy(f32[1024,16]{0,1:T(8,128)} %bitcast.3) | data formatting | bytes 131072

commit v7 on v6

--- a/solution.py
+++ b/solution.py
@@ -16,7 +16,7 @@
 OUTER = 2
 SPAN = 2 * INNER + 1
 TURNS = 2 * OUTER + 1
-CHUNKS = 4
+CHUNKS = 3
 
 
 def circle_fit():
@@ -71,21 +71,21 @@
 
 
 def kernel(
-    scale, tm_count, chan_count, bins_in, slow_in, coords_in, records_ref, out_ref,
+    scale, sizes, tm_count, chan_count, bins_in, slow_in, coords_in, records_ref, out_ref,
     bins_ref, slow_ref, coords_ref,
     blocks, table, stage, send, recv, digits, all_digits, positions,
     yt, yj, c0, s0, c1, s1, sets, dots, power, place, onehot, mine, swapped,
     load_sem, small_sems, halo_sems, digit_sems, send_sems, recv_sems, power_sems,
 ):
     devices = tm_count * chan_count
-    chunks, _, chunk_rows, _ = recv.shape
+    chunks = len(sizes)
+    begins = [sum(sizes[:k]) for k in range(chunks)]
     ch_dev, local_samples = records_ref.shape
     hop = W // 2
     snaps = local_samples // hop
     tiles = snaps * ch_dev // LANES
     per_dev = bins_ref.shape[0] // devices
-    per_chunk = per_dev // chunks
-    freq_rows = table.shape[0]
+    bin_rows = 2 * tiles
     half = LANES // 2
     side = tm_count * 2 * tiles
     my_chan, my_tm = lax.axis_index("chan"), lax.axis_index("tm")
@@ -169,7 +169,7 @@
             values = jnp.zeros((16, 1), jnp.float32)
             for i in range(8):
                 b = r * 8 + i
-                index = lax.div(b, per_chunk) * per_dev + k * per_chunk + lax.rem(b, per_chunk)
+                index = lax.div(b, sizes[k]) * per_dev + begins[k] + lax.rem(b, sizes[k])
                 values = jnp.where(row16 // 2 == i, bins_ref[index].astype(jnp.float32), values)
             turn = values * offset + quarter
             turn = turn - jnp.floor(turn + 0.5)
@@ -177,14 +177,16 @@
             table[rows, :] = (weight * horner(turn * turn, COS_FIT)).astype(table.dtype)
             return 0
 
-        lax.fori_loop(0, freq_rows // 16, table_rows, 0)
+        lax.fori_loop(0, 2 * devices * sizes[k] // 16, table_rows, 0)
 
     table_chunk(0)
     whole = blocks.at[0 : snaps * ch_dev, :]
     pltpu.make_async_copy(whole, whole, load_sem).wait()
 
-    def part(d):
-        return pl.ds(pl.multiple_of(d * chunk_rows, chunk_rows), chunk_rows)
+    def part(k, d, base=True):
+        start = devices * begins[k] * bin_rows if base else 0
+        rows = sizes[k] * bin_rows
+        return pl.ds(pl.multiple_of(start + d * rows, bin_rows), rows)
 
     def partner(j):
         if devices & (devices - 1):
@@ -195,9 +197,11 @@
             other = other + lax.rem(lax.div(j, 2**b), 2) * flip * 2**b
         return other
 
-    def send_chunk(k, _):
+    def send_chunk(k):
+        freq_rows = 2 * devices * sizes[k]
+
         def transform(i, _):
-            @pl.when(jnp.logical_and(k == 0, i == tiles // 2 - 1))
+            @pl.when(i == (tiles // 2 - 1 if k == 0 else -1))
             def _():
                 halo.wait()
                 tail = blocks[snaps * ch_dev :, :]
@@ -207,7 +211,8 @@
             start = pl.multiple_of(i * 2 * LANES, 2 * LANES)
             here = blocks[pl.ds(start, 2 * LANES), :]
             after = blocks[pl.ds(start + ch_dev, 2 * LANES), :]
-            out = product(table[:, :hop], here) + product(table[:, hop:], after)
+            out = product(table[:freq_rows, :hop], here)
+            out += product(table[:freq_rows, hop:], after)
             for j in range(2):
                 rows = pl.ds(2 * i + j, freq_rows, stride=tiles)
                 stage[rows, :] = out[:, j * LANES : (j + 1) * LANES]
@@ -216,7 +221,7 @@
         lax.fori_loop(0, tiles // 2, transform, 0)
 
         def pack(d, _):
-            send[k, part(d), :] = stage[part(d), :].astype(send.dtype)
+            send[part(k, d), :] = stage[part(k, d, False), :].astype(send.dtype)
             return 0
 
         lax.fori_loop(0, devices, pack, 0)
@@ -224,8 +229,8 @@
         def send_one(j, _):
             other = partner(j // 2 + lax.rem(j, 2) * (devices // 2))
             pltpu.make_async_remote_copy(
-                src_ref=send.at[k, part(other), :],
-                dst_ref=recv.at[k, me],
+                src_ref=send.at[part(k, other), :],
+                dst_ref=recv.at[part(k, me), :],
                 send_sem=send_sems.at[k],
                 recv_sem=recv_sems.at[k],
                 device_id=(lax.div(other, tm_count), lax.rem(other, tm_count)),
@@ -234,15 +239,12 @@
             return 0
 
         lax.fori_loop(1, devices, send_one, 0)
-        recv[k, me] = send[k, part(me), :]
-
-        @pl.when(k + 1 < chunks)
-        def _():
+        recv[part(k, me), :] = send[part(k, me), :]
+        if k + 1 < chunks:
             table_chunk(k + 1)
 
-        return 0
-
-    lax.fori_loop(0, chunks, send_chunk, 0)
+    for k in range(chunks):
+        send_chunk(k)
 
     point, spot = grid_place(slow_ref[...])
     place[...] = point
@@ -269,7 +271,7 @@
     step = (lax.broadcasted_iota(jnp.int32, (REACH, 1), 0) + 1).astype(jnp.float32)
 
     def one_bin(k, local, _):
-        f = k * per_chunk + local
+        f = begins[k] + local
         bin_value = bins_ref[me * per_dev + f].astype(jnp.float32)
         for axis, steps, cos_ref, sin_ref in ((0, inner_step, c0, s0), (1, step, c1, s1)):
             turn = positions[axis : axis + 1, :] * bin_value
@@ -285,9 +287,13 @@
             for t in range(tm_count):
                 pairs = []
                 for p in range(2):
-                    rows = pl.ds(pl.multiple_of((2 * local + p) * tiles, tiles), tiles)
-                    left = recv[k, 2 * m * tm_count + t, rows, :].astype(jnp.float32)
-                    right = recv[k, (2 * m + 1) * tm_count + t, rows, :].astype(jnp.float32)
+                    start = devices * begins[k] * bin_rows + (2 * local + p) * tiles
+                    start = pl.multiple_of(start, tiles)
+                    step_rows = sizes[k] * bin_rows
+                    source = 2 * m * tm_count + t
+                    left = recv[pl.ds(start + source * step_rows, tiles), :].astype(jnp.float32)
+                    source += tm_count
+                    right = recv[pl.ds(start + source * step_rows, tiles), :].astype(jnp.float32)
                     even = jnp.where(lane < half, left, pltpu.roll(right, half, 1))
                     odd = jnp.where(lane < half, pltpu.roll(left, half, 1), right)
                     pairs.append((even, odd))
@@ -334,13 +340,14 @@
                 power[pl.ds(f * POINTS + 4 * h + q, 1), :] = total * scale
         return 0
 
-    def one_chunk(k, _):
-        arrived = recv.at[k, 0 : devices - 1]
+    def all_but_one(k):
+        start = devices * begins[k] * bin_rows
+        return pl.ds(start, (devices - 1) * sizes[k] * bin_rows)
+
+    for k in range(chunks):
+        arrived = recv.at[all_but_one(k), :]
         pltpu.make_async_copy(arrived, arrived, recv_sems.at[k]).wait()
-        lax.fori_loop(0, per_chunk, functools.partial(one_bin, k), 0)
-        return 0
-
-    lax.fori_loop(0, chunks, one_chunk, 0)
+        lax.fori_loop(0, sizes[k], functools.partial(one_bin, k), 0)
 
     high = power[...].astype(jnp.bfloat16)
     rest = (power[...] - high.astype(jnp.float32)).astype(jnp.bfloat16)
@@ -372,12 +379,9 @@
         copy.wait()
     out_ref[...] = swapped[...]
 
-    def drain(k, _):
-        sent = send.at[k, 0 : (devices - 1) * chunk_rows, :]
+    for k in range(chunks):
+        sent = send.at[all_but_one(k), :]
         pltpu.make_async_copy(sent, sent, send_sems.at[k]).wait()
-        return 0
-
-    lax.fori_loop(0, chunks, drain, 0)
 
 
 def shards(records, coords, bins, slow_index):
@@ -390,9 +394,10 @@
     channels = ch_dev * chan_count
     freq = bins.shape[0]
     per_dev = freq // devices
-    chunks = math.gcd(per_dev, CHUNKS)
+    chunks = min(per_dev, CHUNKS)
+    sizes = tuple((per_dev + chunks - 1 - k) // chunks for k in range(chunks))
     tiles = snaps * ch_dev // LANES
-    chunk_rows = 2 * per_dev * tiles // chunks
+    most = 2 * devices * max(sizes)
     columns = TURNS * 4 * tm_count * tiles
     kept = 8 * ((per_dev + 7) // 8)
     own = slow_index.shape[1] // tm_count
@@ -401,7 +406,7 @@
     inner_angles = pltpu.VMEM((8, channels), jnp.float32)
     angles = pltpu.VMEM((REACH, channels), jnp.float32)
     power = pl.pallas_call(
-        functools.partial(kernel, scale, tm_count, chan_count),
+        functools.partial(kernel, scale, sizes, tm_count, chan_count),
         out_shape=jax.ShapeDtypeStruct((tm_count, kept, own), jnp.float32),
         in_specs=[pl.BlockSpec(memory_space=pl.ANY)] * 4,
         out_specs=vmem,
@@ -410,10 +415,10 @@
             pltpu.VMEM(slow_index.shape, jnp.int32),
             pltpu.VMEM(coords.shape, jnp.int32),
             pltpu.VMEM(((snaps + 1) * ch_dev, hop), jnp.bfloat16),
-            pltpu.VMEM((2 * freq // chunks, W), jnp.bfloat16),
-            pltpu.VMEM((2 * freq * tiles // chunks, LANES), jnp.float32),
-            pltpu.VMEM((chunks, devices * chunk_rows, LANES), jnp.bfloat16),
-            pltpu.VMEM((chunks, devices, chunk_rows, LANES), jnp.bfloat16),
+            pltpu.VMEM((most, W), jnp.bfloat16),
+            pltpu.VMEM((most * tiles, LANES), jnp.float32),
+            pltpu.VMEM((2 * freq * tiles, LANES), jnp.bfloat16),
+            pltpu.VMEM((2 * freq * tiles, LANES), jnp.bfloat16),
             pltpu.VMEM((16, LANES), jnp.bfloat16),
             pltpu.VMEM((chan_count, 16, LANES), jnp.bfloat16),
             pltpu.VMEM((2, channels), jnp.float32),

time: 67.4 us -> 69.8 us (1.036)
  Pallas kernels: 65.8 us -> 67.9 us
    pallas_call x1, Pallas kernels: 65.8 us -> 67.9 us  [shards(): pl.pallas_call(functools.partial(kernel, scale, sizes, tm_count, chan_cou...]
where the time goes in v7:
time: 69.8 us; the launch traced here: 69.4 us
  Pallas kernels  67.9 us (97%)
  local copies, waits for them, and re-layouts  1.47 us (2%)
    pallas_call x1, Pallas kernels, shards(): pl.pallas_call(functools.partial(kernel, scale, sizes, tm_count, chan_cou...  67.9 us
    unnamed x1, local copies, waits for them, and re-layouts  1.47 us

profile of v7, /device:TPU:10, one launch (start us, length us, event | category | flops | bytes accessed | tf_op | source)
XLA Modules:
  0.0 69.4 jit_solution(17217734934182688641)
XLA Ops:
  0.0 67.9 %shard_map.46 = f32[2,8,1024]{2,1,0:T(8,128)} custom-call(s32[256]{0:T(256)} %bins_in.1, s32[2,2048]{1,0:T(2,128)} %slow_in.1, s32[2,64]{1,0:T(2,128)} %coords_in.1, bf16[64,32768]{1,0:T(8,128)(2,1)} %records_ref.1), custom_call_target="tpu_custom_call" | custom-call | flops 10737418240 | bytes 4194304 | tf_op jit(solution)/shard_map/pallas_call | solution.py:408
  67.9 1.5 %copy.6 = f32[1024,16]{0,1:T(8,128)} copy(f32[1024,16]{0,1:T(8,128)} %bitcast.3) | data formatting | bytes 131072
